TPU v7x, 32 devices: a whole 2x2x4 slice. The times are simulated.
32 devices in a mesh: dp: 16 (over z, y, x), mp: 2 (over core).
Axes of the slice: x: 2, y: 2, z: 4, core: 2. Of those that a mesh axis runs over, the one named last changes fastest.
Arguments:
- tokens_in: bfloat16 [16, 1024, 960], P('dp'), may hold values from -6 to 6
- segment_ids: int32 [16, 1024], P('dp'), may hold values from 0 to 7, never falling along the last dimension, each value on 1 to 512 neighbouring positions
- kv_owner: int32 [5], replicated, may hold values from 0 to 1, as said below
- w_query: bfloat16 [5, 960, 192], replicated, may hold values from -0.1875 to 0.1875
- w_key: bfloat16 [5, 960, 64], replicated, may hold values from -0.1875 to 0.1875
- w_value: bfloat16 [5, 960, 64], replicated, may hold values from -0.1875 to 0.1875
- w_out: bfloat16 [5, 192, 960], replicated, may hold values from -1.5 to 1.5
- attn_gain: bfloat16 [960], replicated, may hold values from 0.099609375 to 1.8984375
- w_gate: bfloat16 [960, 2560], P(None, 'mp'), may hold values from -0.1875 to 0.1875
- w_up: bfloat16 [960, 2560], P(None, 'mp'), may hold values from -0.1875 to 0.1875
- w_down: bfloat16 [2560, 960], P('mp'), may hold values from -0.125 to 0.125
- ffn_gain: bfloat16 [960], replicated, may hold values from 0.099609375 to 1.8984375
- cotangent: bfloat16 [16, 1024, 960], P('dp'), may hold values from -6 to 6
Outputs:
- tokens_out: bfloat16 [16, 1024, 960], P('dp')
- grad_in: float32 [16, 1024, 960], P('dp')
- grad_query: float32 [6, 960, 192], P('mp', 'dp')
- grad_key: float32 [6, 960, 64], P('mp', 'dp')
- grad_value: float32 [6, 960, 64], P('mp', 'dp')
- grad_out: float32 [6, 192, 960], P('mp', None, 'dp')
- grad_gate: float32 [960, 2560], P('dp', 'mp')
- grad_up: float32 [960, 2560], P('dp', 'mp')
- grad_down: float32 [2560, 960], P('mp', 'dp')
- grad_attn_gain: float32 [960], P('dp')
- grad_ffn_gain: float32 [960], P('dp')
Inputs may be any that keep to these rules, and one draw needn't show every extreme that they name: Group g is worked on by the mp device kv_owner[g]; one device holds 3 groups, the other the remaining ones.
All inputs are finite; a program needn't handle non-finite values.
Results may differ from a plain program's by a relative error of at most 0.03.
Values may be sent and summed in bfloat16 or wider, within the bound.
No kernel may reach another device: no remote copies, remote signals or barrier semaphores. Data moves between devices by JAX's collectives and lax.ppermute only.
A program may use at most 320 MiB of HBM per device.

v0:
```python
import functools
import math

import jax
import jax.numpy as jnp
import numpy as np
from jax import lax
from jax.experimental import pallas as pl
from jax.experimental.pallas import tpu as pltpu
from jax.sharding import PartitionSpec as P

REPEAT = 2
BLOCK = 256
FFN_BLOCK = 512
LANES = 128
HEAD = 64
GROUP = 3
VROWS = 80
epsilon = 1e-05
masked_value = -1e30
LOG2E = math.log2(math.e)
LN2 = math.log(2.0)
f32 = jnp.float32
bf16 = jnp.bfloat16
NN = (((1,), (0,)), ((), ()))
NT = (((1,), (1,)), ((), ()))
TN = (((0,), (0,)), ((), ()))
MIB = 1024 * 1024


def matmul(a, b, dims=NN):
    return lax.dot_general(a, b, dims, preferred_element_type=f32)


def wide(column, width):
    return jnp.concatenate([column] * (width // LANES), axis=1)


def inverse_rms(values):
    return lax.rsqrt(jnp.mean(values * values, axis=0, keepdims=True) + epsilon)


def normalise(values, gain, inverse_out):
    inverse = inverse_rms(values)
    inverse_out[...] = inverse
    return (values * inverse * wide(gain, values.shape[1])).astype(bf16)


def norm_back(normed, inverse, gain, grad_normed):
    normed = normed.astype(f32)
    inner_mean = jnp.mean(grad_normed * normed, axis=0, keepdims=True)
    width = normed.shape[1]
    return inverse * (grad_normed * wide(gain, width) - normed * wide(1.0 / gain, width) * inner_mean)


def joined_sum(own_ref, other_ref):
    return own_ref[...].astype(f32) + other_ref[...].astype(f32)


def three_parts(value):
    high = value.astype(bf16).astype(f32)
    rest = value - high
    middle = rest.astype(bf16).astype(f32)
    return high, middle, rest - middle


def part_rows(value, first):
    row = lax.broadcasted_iota(jnp.int32, (8, value.shape[1]), 0)
    out = jnp.zeros((8, value.shape[1]), f32)
    for number, part in enumerate(three_parts(value)):
        out = jnp.where(row == first + number, part, out)
    return out


def causal_bias(heads):
    key = lax.broadcasted_iota(jnp.int32, (BLOCK, heads * BLOCK), 0)
    query = lax.broadcasted_iota(jnp.int32, (BLOCK, heads * BLOCK), 1) % BLOCK
    return jnp.where(key <= query, 0.0, masked_value)


def reaches(segments, step, back):
    last = jnp.maximum((step - back + 1) * BLOCK - 1, 0)
    return (step >= back) & (segments[last] == segments[step * BLOCK])


def block_at(index):
    return pl.ds(pl.multiple_of(index * BLOCK, BLOCK), BLOCK)


def turn(upper, lower, cosine, sine):
    return upper * cosine - lower * sine, lower * cosine + upper * sine


def attention_forward(joined, slots, heads, segments, *refs):
    refs = list(refs)
    hidden = refs.pop(0)[...].astype(f32)
    if joined:
        hidden = hidden + joined_sum(refs.pop(0), refs.pop(0))
    gain_ref, wqkv_ref, wout_ref, cos_ref, sin_ref, segment_ref = refs[:6]
    refs = refs[6:]
    if joined:
        refs.pop(0)[...] = hidden
    (normed_out, inverse_out, query_out, key_out, turned_key_out, value_out, attended_out, partial_out,
     turned_value, tri_ref) = refs
    step = pl.program_id(0)
    here = block_at(step)

    @pl.when(step == 0)
    def _():
        tri_ref[...] = causal_bias(heads)

    normed = normalise(hidden, gain_ref[...], inverse_out)
    normed_out[...] = normed
    projected = matmul(wqkv_ref[...], normed)
    cosine, sine = cos_ref[...], sin_ref[...]
    half = HEAD // 2

    same = lax.broadcasted_iota(jnp.int32, (8, BLOCK), 0) == segment_ref[...]
    query_rows = jnp.where(same, 1.0, 0.0)
    key_rows = jnp.where(same, 0.0, masked_value)
    row = lax.broadcasted_iota(jnp.int32, (8, BLOCK), 0)
    minus_rows = jnp.where(row < 3, -1.0, 0.0)
    scale = LOG2E / math.sqrt(HEAD)
    query_fill = jnp.concatenate(
        [query_rows, jnp.zeros((LANES - HEAD - 8, BLOCK), f32)], axis=0
    ).astype(bf16)

    for s in range(slots):
        for j in range(heads + 2):
            first = (s * (heads + 2) + j) * HEAD
            piece = projected[first : first + HEAD]
            if j > heads:
                value = jnp.concatenate([piece, jnp.ones((LANES - HEAD, BLOCK), f32)], axis=0)
                value_out[here, s * LANES : (s + 1) * LANES] = value.T.astype(bf16)
                turned_value[s * VROWS : (s + 1) * VROWS, here] = value[:VROWS].astype(bf16)
                continue
            upper, lower = turn(piece[:half], piece[half:], cosine, sine)
            if j < heads:
                lanes = slice(j * BLOCK, (j + 1) * BLOCK)
                query_out[0, s, :HEAD, lanes] = jnp.concatenate(
                    [upper * scale, lower * scale], axis=0
                ).astype(bf16)
                query_out[0, s, HEAD:, lanes] = query_fill
            else:
                turned_key_out[s * HEAD : (s + 1) * HEAD, :] = jnp.concatenate(
                    [upper, lower], axis=0
                ).astype(bf16)
                whole = jnp.concatenate(
                    [upper, lower, key_rows, minus_rows, jnp.zeros((LANES - HEAD - 16, BLOCK), f32)],
                    axis=0,
                )
                key_out[here, s * LANES : (s + 1) * LANES] = whole.T.astype(bf16)

    query_rows = jnp.concatenate([query_rows] * heads, axis=1)

    def attend(blocks):
        width = blocks * BLOCK
        keys = pl.ds(pl.multiple_of((step + 1 - blocks) * BLOCK, BLOCK), width)
        scores = [
            matmul(key_out[keys, s * LANES : (s + 1) * LANES], query_out[0, s]) for s in range(slots)
        ]
        tops, weights = [], []
        for score in scores:
            last = score[width - BLOCK :] + tri_ref[...]
            if blocks > 1:
                score = jnp.concatenate([score[: width - BLOCK], last], axis=0)
            else:
                score = last
            tops.append(jnp.max(score, axis=0, keepdims=True))
            weights.append(jnp.exp2(score - tops[-1]).astype(bf16))
        summed = [
            matmul(turned_value[s * VROWS : (s + 1) * VROWS, keys], weights[s]) for s in range(slots)
        ]
        for s in range(slots):
            weight_sum = summed[s][HEAD : HEAD + 1]
            out = (summed[s][:HEAD] * (1.0 / weight_sum)).astype(bf16)
            for j in range(heads):
                first = (s * heads + j) * HEAD
                attended_out[first : first + HEAD, :] = out[:, j * BLOCK : (j + 1) * BLOCK]
            query_out[0, s, HEAD : HEAD + 16, :] = jnp.concatenate(
                [query_rows, part_rows(tops[s] + jnp.log2(weight_sum), 0)], axis=0
            ).astype(bf16)

    one = reaches(segments, step, 1)
    two = reaches(segments, step, 2)
    pl.when(jnp.logical_not(one))(functools.partial(attend, 1))
    pl.when(one & jnp.logical_not(two))(functools.partial(attend, 2))
    pl.when(two)(functools.partial(attend, 3))
    partial_out[...] = matmul(wout_ref[...], attended_out[...], TN).astype(bf16)


def chunks(width):
    return [slice(start, start + 256) for start in range(0, width, 256)]


def cost(flops, *arrays):
    size = sum(math.prod(a.shape) * a.dtype.itemsize for a in arrays)
    return pl.CostEstimate(flops=int(flops), bytes_accessed=size, transcendentals=0)


def token_spec(rows, width=BLOCK):
    return pl.BlockSpec((rows, width), lambda i, *_: (0, i))


def unit_shape(units, length):
    return shape_of((length // FFN_BLOCK, units, FFN_BLOCK), bf16)


def unit_spec(units):
    return pl.BlockSpec((1, units, FFN_BLOCK), lambda i: (i, 0, 0))


def full_spec(shape):
    return pl.BlockSpec(
        shape, lambda *_: (0,) * len(shape), pipeline_mode=pl.Buffered(buffer_count=1)
    )


def out_full_spec(shape):
    return pl.BlockSpec(shape, lambda *_: (0,) * len(shape))


shape_of = pltpu.HBM
anywhere = jax.ShapeDtypeStruct


def in_hbm(*arrays):
    return tuple(pltpu.with_memory_space_constraint(array, pltpu.HBM) for array in arrays)


def call_attention_forward(segments, parts, gain, wqkv, wout, cosine, sine, slots, heads):
    features, length = parts[0].shape
    joined = len(parts) == 3
    total = slots * heads
    big = shape_of((features, length), bf16)
    outs = [
        (big, token_spec(features)),
        (shape_of((1, length), f32), token_spec(1)),
        (
            shape_of((length // BLOCK, slots, LANES, heads * BLOCK), bf16),
            pl.BlockSpec((1, slots, LANES, heads * BLOCK), lambda i, *_: (i, 0, 0, 0)),
        ),
        (shape_of((length, slots * LANES), bf16), out_full_spec((length, slots * LANES))),
        (shape_of((slots * HEAD, length), bf16), token_spec(slots * HEAD)),
        (shape_of((length, slots * LANES), bf16), out_full_spec((length, slots * LANES))),
        (shape_of((total * HEAD, length), bf16), token_spec(total * HEAD)),
        (anywhere((features, length), bf16), token_spec(features)),
    ]
    if joined:
        outs.insert(0, (shape_of((features, length), f32), token_spec(features)))
    return pl.pallas_call(
        functools.partial(attention_forward, joined, slots, heads),
        grid_spec=pltpu.PrefetchScalarGridSpec(
            num_scalar_prefetch=1,
            grid=(length // BLOCK,),
            in_specs=[token_spec(features)] * len(parts)
            + [full_spec(a.shape) for a in (gain, wqkv, wout)]
            + [token_spec(HEAD // 2)] * 2
            + [token_spec(1)],
            out_specs=[spec for _, spec in outs],
            scratch_shapes=[
                pltpu.VMEM((slots * VROWS, length), bf16),
                pltpu.VMEM((BLOCK, heads * BLOCK), f32),
            ],
        ),
        out_shape=[shape for shape, _ in outs],
        compiler_params=pltpu.CompilerParams(vmem_limit_bytes=32 * MIB),
        cost_estimate=cost(2 * length * features * (wqkv.shape[0] + wout.shape[0]) + 12e9, *parts),
        name="attention_forward",
    )(segments, *in_hbm(parts[0]), *parts[1:], gain, wqkv, wout, cosine, sine, segments[None, :])


def ffn_forward(hidden_ref, own_ref, other_ref, gain_ref, gate_ref, up_ref, down_ref,
                middle_out, normed_out, inverse_out, gate_out, lift_out, inner_out, partial_out):
    middle = hidden_ref[...].astype(f32) + joined_sum(own_ref, other_ref)
    middle_out[...] = middle
    normed = normalise(middle, gain_ref[...], inverse_out)
    normed_out[...] = normed
    for chunk in chunks(gate_ref.shape[1]):
        gate = matmul(gate_ref[:, chunk], normed, TN)
        lift = matmul(up_ref[:, chunk], normed, TN)
        gate_out[0, chunk, :] = gate.astype(bf16)
        lift_out[0, chunk, :] = lift.astype(bf16)
        inner_out[0, chunk, :] = (gate * jax.nn.sigmoid(gate) * lift).astype(bf16)
    partial_out[...] = matmul(down_ref[...], inner_out[0]).astype(bf16)


def call_ffn_forward(hidden, own, other, gain, w_gate, w_up, w_down):
    features, length = hidden.shape
    units = w_gate.shape[1]
    spec = functools.partial(token_spec, width=FFN_BLOCK)
    return pl.pallas_call(
        ffn_forward,
        grid=(length // FFN_BLOCK,),
        in_specs=[spec(features)] * 3 + [full_spec(a.shape) for a in (gain, w_gate, w_up, w_down)],
        out_specs=[spec(features)] * 2 + [spec(1)] + [unit_spec(units)] * 3 + [spec(features)],
        out_shape=[
            shape_of((features, length), f32), shape_of((features, length), bf16),
            shape_of((1, length), f32), *[unit_shape(units, length)] * 3,
            anywhere((features, length), bf16),
        ],
        compiler_params=pltpu.CompilerParams(vmem_limit_bytes=40 * MIB),
        cost_estimate=cost(6 * length * features * units, hidden),
        name="ffn_forward",
    )(*in_hbm(hidden), own, other, gain, w_gate, w_up, w_down)


def ffn_backward(joined, grad_ref, *refs):
    grad = grad_ref[...]
    if joined:
        normed_ref, inverse_ref, own_ref, other_ref, gain_ref = refs[:5]
        refs = refs[5:]
        back = norm_back(normed_ref[...], inverse_ref[...], gain_ref[...], joined_sum(own_ref, other_ref))
        grad = (grad.astype(f32) + back).astype(bf16)
    gate_in, lift_in, gate_ref, up_ref, down_ref = refs[:5]
    refs = refs[5:]
    if joined:
        refs[0][...] = grad
        refs = refs[1:]
    grad_gate_out, grad_lift_out, partial_out = refs
    for chunk in chunks(gate_ref.shape[1]):
        grad_inner = matmul(down_ref[:, chunk], grad, TN)
        gate = gate_in[0, chunk, :].astype(f32)
        lift = lift_in[0, chunk, :].astype(f32)
        sigmoid = jax.nn.sigmoid(gate)
        grad_gate = grad_inner * lift * sigmoid * (1.0 + gate * (1.0 - sigmoid))
        grad_gate_out[0, chunk, :] = grad_gate.astype(bf16)
        grad_lift_out[0, chunk, :] = (grad_inner * gate * sigmoid).astype(bf16)
    partial = matmul(gate_ref[...], grad_gate_out[0]) + matmul(up_ref[...], grad_lift_out[0])
    partial_out[...] = partial.astype(bf16)


def call_ffn_backward(grad, joint, gate, lift, w_gate, w_up, w_down):
    features, length = grad.shape
    units = w_gate.shape[1]
    spec = functools.partial(token_spec, width=FFN_BLOCK)
    joint_specs, extra = [], []
    if joint:
        normed, inverse, own, other, gain = joint
        joint = (*in_hbm(normed), inverse, own, other, gain)
        joint_specs = [spec(features), spec(1), spec(features), spec(features), full_spec(gain.shape)]
        extra = [(shape_of((features, length), bf16), spec(features))]
    outs = extra + [(unit_shape(units, length), unit_spec(units))] * 2
    outs.append((anywhere((features, length), bf16), spec(features)))
    return pl.pallas_call(
        functools.partial(ffn_backward, bool(joint)),
        grid=(length // FFN_BLOCK,),
        in_specs=[spec(features)] + joint_specs + [unit_spec(units)] * 2
        + [full_spec(a.shape) for a in (w_gate, w_up, w_down)],
        out_specs=[spec for _, spec in outs],
        out_shape=[shape for shape, _ in outs],
        compiler_params=pltpu.CompilerParams(vmem_limit_bytes=40 * MIB),
        cost_estimate=cost(6 * length * features * units, grad),
        name="ffn_backward",
    )(*in_hbm(grad), *joint, *in_hbm(gate, lift), w_gate, w_up, w_down)


def attention_backward(slots, heads, segments, grad_ref, own_ref, other_ref, normed_ref, inverse_ref,
                       gain_ref, wout_ref, wqkv_ref, attended_ref, query_ref, key_ref, turned_key_ref,
                       value_ref, cos_ref, sin_ref,
                       attn_grad_out, projected_out, partial_out,
                       key_total, value_total, query_total, grad_heads, tri_ref):
    step = pl.num_programs(0) - 1 - pl.program_id(0)
    half = HEAD // 2

    @pl.when(pl.program_id(0) == 0)
    def _():
        key_total[...] = jnp.zeros_like(key_total)
        value_total[...] = jnp.zeros_like(value_total)
        tri_ref[...] = causal_bias(heads)

    back = norm_back(normed_ref[...], inverse_ref[...], gain_ref[...], joined_sum(own_ref, other_ref))
    attn_grad = (grad_ref[...].astype(f32) + back).astype(bf16)
    attn_grad_out[...] = attn_grad
    grad_attended = matmul(wout_ref[...], attn_grad).astype(bf16)
    zeros = jnp.zeros((LANES - HEAD - 8, BLOCK), f32)
    for s in range(slots):
        for j in range(heads):
            first = (s * heads + j) * HEAD
            mine = grad_attended[first : first + HEAD]
            out = attended_ref[first : first + HEAD, :]
            delta = jnp.sum(mine.astype(f32) * out.astype(f32), axis=0, keepdims=True)
            lanes = slice(j * BLOCK, (j + 1) * BLOCK)
            grad_heads[s, :HEAD, lanes] = mine
            grad_heads[s, HEAD:, lanes] = jnp.concatenate(
                [part_rows(-delta, 0), zeros], axis=0
            ).astype(bf16)

    def visit(back):
        keys = block_at(step - back)
        columns = [slice(s * LANES, (s + 1) * LANES) for s in range(slots)]
        features = [slice(s * HEAD, (s + 1) * HEAD) for s in range(slots)]
        scores = [matmul(key_ref[keys, columns[s]], query_ref[0, s]) for s in range(slots)]
        grad_weights = [matmul(value_ref[keys, columns[s]], grad_heads[s]) for s in range(slots)]
        weights, grad_scores = [], []
        for s in range(slots):
            score = scores[s] + tri_ref[...] if back == 0 else scores[s]
            weight = jnp.exp2(score)
            weights.append(weight.astype(bf16))
            grad_scores.append((weight * grad_weights[s]).astype(bf16))
        for s in range(slots):
            value_total[features[s], keys] += matmul(grad_heads[s, :HEAD, :], weights[s], NT)
            key_total[features[s], keys] += matmul(query_ref[0, s, :HEAD, :], grad_scores[s], NT)
            update = matmul(turned_key_ref[features[s], keys], grad_scores[s])
            if back == 0:
                query_total[s] = update
            else:
                query_total[s] += update

    visit(0)
    for back in (1, 2):
        pl.when(reaches(segments, step, back))(functools.partial(visit, back))

    cosine, sine = cos_ref[...], sin_ref[...]
    here = block_at(step)
    for s in range(slots):
        for j in range(heads + 2):
            if j < heads:
                piece = query_total[s, :, j * BLOCK : (j + 1) * BLOCK] * (1.0 / math.sqrt(HEAD))
            elif j == heads:
                piece = key_total[s * HEAD : (s + 1) * HEAD, here] * LN2
            else:
                piece = value_total[s * HEAD : (s + 1) * HEAD, here]
            if j <= heads:
                upper, lower = turn(piece[:half], piece[half:], cosine, -sine)
                piece = jnp.concatenate([upper, lower], axis=0)
            first = (s * (heads + 2) + j) * HEAD
            projected_out[first : first + HEAD, :] = piece.astype(bf16)
    partial_out[...] = matmul(wqkv_ref[...], projected_out[...], TN).astype(bf16)


def call_attention_backward(segments, grad, own, other, normed, inverse, gain, wout, wqkv, attended, query,
                            key, turned_key, value, cosine, sine):
    features, length = grad.shape
    count = length // BLOCK
    slots, wide_heads = query.shape[1], query.shape[3]
    heads = wide_heads // BLOCK

    def spec(rows):
        return pl.BlockSpec((rows, BLOCK), lambda i, *_: (0, count - 1 - i))

    return pl.pallas_call(
        functools.partial(attention_backward, slots, heads),
        grid_spec=pltpu.PrefetchScalarGridSpec(
            num_scalar_prefetch=1,
            grid=(count,),
            in_specs=[spec(features)] * 4 + [spec(1)]
            + [full_spec(a.shape) for a in (gain, wout, wqkv)]
            + [spec(attended.shape[0])]
            + [pl.BlockSpec((1, slots, LANES, wide_heads), lambda i, *_: (count - 1 - i, 0, 0, 0))]
            + [full_spec(a.shape) for a in (key, turned_key, value)]
            + [spec(HEAD // 2)] * 2,
            out_specs=[spec(features), spec(wqkv.shape[0]), spec(features)],
            scratch_shapes=[
                pltpu.VMEM((slots * HEAD, length), f32),
                pltpu.VMEM((slots * HEAD, length), f32),
                pltpu.VMEM((slots, HEAD, wide_heads), f32),
                pltpu.VMEM((slots, LANES, wide_heads), bf16),
                pltpu.VMEM((BLOCK, wide_heads), f32),
            ],
        ),
        out_shape=[
            shape_of((features, length), bf16), shape_of((wqkv.shape[0], length), bf16),
            anywhere((features, length), bf16),
        ],
        compiler_params=pltpu.CompilerParams(vmem_limit_bytes=30 * MIB),
        cost_estimate=cost(2 * length * features * (wqkv.shape[0] + wout.shape[0]) + slots * 8e9, grad),
        name="attention_backward",
    )(segments, *in_hbm(grad), own, other, *in_hbm(normed), inverse, gain, wout, wqkv,
      *in_hbm(attended, query), key, turned_key, value, cosine, sine)


def shard_rows(total, out_ref, order, rows, mine, first=0):
    total = total.astype(bf16)
    columns = slice(first, first + total.shape[1])
    half = len(order) // 2
    for place, shard in enumerate(order):
        side = mine if place < half else 1 - mine
        out_ref[side, place % half, :rows, columns] = total[shard * rows : (shard + 1) * rows]
        if out_ref.shape[2] > rows:
            out_ref[side, place % half, rows:, columns] = jnp.zeros(
                (out_ref.shape[2] - rows, total.shape[1]), bf16
            )


def begin_sending(staged, kept, sent, kept_signal, sent_signal):
    copies = [
        pltpu.make_async_copy(staged.at[1], sent, sent_signal),
        pltpu.make_async_copy(staged.at[0], kept, kept_signal),
    ]
    begin(copies)
    return copies


def fetches(pairs, arrived):
    groups, count = [], 0
    for sources, target in pairs:
        parts = []
        for source in sources:
            parts += [source] if len(source.shape) == 2 else [source.at[i] for i in range(source.shape[0])]
        first, group = 0, []
        for part in parts:
            lanes = target.at[:, pl.ds(first, part.shape[1])]
            group.append(pltpu.make_async_copy(part, lanes, arrived.at[count]))
            first += part.shape[1]
            count += 1
        groups.append(group)
    return groups


def begin(copies):
    for copy in copies:
        copy.start()


def finish(copies):
    for copy in copies:
        copy.wait()


def halves_product(left, right, copies):
    length = left.shape[1] // 2
    finish(copies[:2])
    total = matmul(left[:, :length], right[:, :length], NT)
    finish(copies[2:])
    return total + matmul(left[:, length:], right[:, length:], NT)


def ffn_weight_grad(orders, rows, bits, *refs):
    sources, outs = refs[:10], refs[10:16]
    buffers, staged, arrived, left = refs[16:21], refs[21], refs[22], refs[23]
    copies = fetches([(sources[2 * i : 2 * i + 2], buffers[i]) for i in range(5)], arrived)
    normed, gates, lifts, grads, inners = buffers
    begin(copies[0] + copies[1])
    outgoing = []

    def write(number, product):
        slot = number % 2
        if number >= 2:
            finish(outgoing[number - 2])
        for chunk in chunks(staged.shape[4]):
            shard_rows(product(chunk), staged.at[slot], orders[number], rows, bits[number], chunk.start)
        outgoing.append(
            begin_sending(
                staged.at[slot], outs[2 * number], outs[2 * number + 1],
                left.at[2 * number], left.at[2 * number + 1],
            )
        )

    finish(copies[0] + copies[1])
    begin(copies[2] + copies[3] + copies[4])
    write(0, lambda chunk: matmul(normed[...], gates[chunk, :], NT))
    finish(copies[2])
    write(1, lambda chunk: matmul(normed[...], lifts[chunk, :], NT))
    finish(copies[3] + copies[4])
    write(2, lambda chunk: matmul(grads[...], inners[chunk, :], NT))
    for pair in outgoing[1:]:
        finish(pair)


def call_weight_grad(kernel, name, bits, pairs, orders, columns, stages, flops):
    features, length = pairs[0][0].shape
    arrivals = sum(len(pair) * (1 if pair[0].ndim == 2 else pair[0].shape[0]) for pair in pairs)
    size = len(orders[0])
    rows = features // size
    padded = -(-rows // 16) * 16
    out = (size // 2, padded, columns)
    outs = pl.pallas_call(
        functools.partial(kernel, orders, rows),
        grid_spec=pltpu.PrefetchScalarGridSpec(
            num_scalar_prefetch=1,
            grid=(1,),
            in_specs=[pl.BlockSpec(memory_space=pl.ANY)] * (2 * len(pairs)),
            out_specs=[pl.BlockSpec(memory_space=pl.ANY)] * (2 * len(orders)),
            scratch_shapes=[pltpu.VMEM((pair[0].shape[-2], 2 * length), bf16) for pair in pairs]
            + [pltpu.VMEM((stages, 2) + out, bf16)]
            + [pltpu.SemaphoreType.DMA((arrivals,)), pltpu.SemaphoreType.DMA((2 * len(orders),))],
        ),
        out_shape=[shape_of(out, bf16)] * (2 * len(orders)),
        compiler_params=pltpu.CompilerParams(vmem_limit_bytes=52 * MIB),
        cost_estimate=cost(flops, *(array for pair in pairs for array in pair)),
        name=name,
    )(bits, *in_hbm(*(array for pair in pairs for array in pair)))
    return list(zip(outs[::2], outs[1::2]))


def call_ffn_weight_grad(bits, normed, grads, rights, orders):
    units = rights[0][0].shape[1]
    pairs = (normed, rights[0], rights[1], grads, rights[2])
    flops = 12 * normed[0].shape[0] * normed[0].shape[1] * units
    return call_weight_grad(ffn_weight_grad, "ffn_weight_grad", bits, pairs, orders, units, 2, flops)


def attention_weight_grad(orders, rows, bits, *refs):
    sources, outs = refs[:8], refs[8:14]
    buffers, staged, arrived, left = refs[14:18], refs[18], refs[19], refs[20]
    copies = fetches([(sources[2 * i : 2 * i + 2], buffers[i]) for i in range(4)], arrived)
    begin(copies[0] + copies[1])
    outgoing = []
    width = staged.shape[4]

    def write(number, pieces):
        column = 0
        for piece in pieces:
            shard_rows(piece, staged.at[number], orders[number], rows, bits[number], column)
            column += piece.shape[1]
        outgoing.extend(
            begin_sending(
                staged.at[number], outs[2 * number], outs[2 * number + 1],
                left.at[2 * number], left.at[2 * number + 1],
            )
        )

    def project(start, stop):
        return matmul(buffers[0][...], buffers[1][start:stop, :], NT)

    def outward(start, stop):
        return matmul(buffers[2][...], buffers[3][start:stop, :], NT)

    columns, most = buffers[1].shape[0], buffers[3].shape[0]
    rest = 2 * width - columns
    finish(copies[0] + copies[1])
    begin(copies[2] + copies[3])
    write(0, [project(start, start + 256) for start in range(0, width, 256)])
    body, tail = project(width, width + 256), project(width + 256, columns)
    finish(copies[2] + copies[3])
    write(1, [body, jnp.concatenate([tail, outward(0, rest)], axis=1)])
    write(2, [outward(start, min(start + 256, most)) for start in range(rest, most, 256)])
    finish(outgoing)


def call_attention_weight_grad(bits, above, below, orders):
    columns = above[1].shape[0] + above[3].shape[0]
    flops = 4 * above[0].shape[0] * above[0].shape[1] * columns
    return call_weight_grad(
        attention_weight_grad, "attention_weight_grad", bits, list(zip(above, below)), orders,
        columns // len(orders), len(orders), flops,
    )


def block_grad(grad_ref, normed_ref, inverse_ref, own_ref, other_ref, gain_ref, out_ref):
    back = norm_back(normed_ref[...], inverse_ref[...], gain_ref[...], joined_sum(own_ref, other_ref))
    out_ref[...] = (grad_ref[...].astype(f32) + back).astype(out_ref.dtype)


def call_block_grad(grad, normed, inverse, own, other, gain, kind):
    features, length = grad.shape
    spec = functools.partial(token_spec, width=FFN_BLOCK)
    return pl.pallas_call(
        block_grad,
        grid=(length // FFN_BLOCK,),
        in_specs=[spec(features)] * 2 + [spec(1)] + [spec(features)] * 2 + [full_spec(gain.shape)],
        out_specs=spec(features),
        out_shape=shape_of((features, length), kind),
        compiler_params=pltpu.CompilerParams(vmem_limit_bytes=32 * MIB),
        cost_estimate=cost(0, grad, normed, own, other),
        name="block_grad",
    )(*in_hbm(grad, normed), inverse, own, other, gain)


def gather_groups(owner, device, *refs):
    sources, (wqkv_out, wout_out), arrived = refs[:4], refs[4:6], refs[6]
    heights = [source.shape[1] for source in sources]
    joint = sum(heights[:3])
    slots = wqkv_out.shape[0] // joint
    for action in ("start", "wait"):
        for slot in range(slots):
            group, held = group_of(slot, owner, device)
            first = slot * joint
            for place, (source, height) in enumerate(zip(sources, heights)):
                if place < 3:
                    target = wqkv_out.at[pl.ds(first, height)]
                    first += height
                else:
                    target = wout_out.at[pl.ds(slot * height, height)]
                copy = pltpu.make_async_copy(source.at[group], target, arrived.at[4 * slot + place])

                def empty(target=target):
                    target[...] = jnp.zeros(target.shape, bf16)

                pl.when(held)(getattr(copy, action))
                if action == "start":
                    pl.when(jnp.logical_not(held))(empty)


def group_of(slot, owner, device):
    found, count = 0, 0
    for group in range(owner.shape[0]):
        mine = owner[group] == device[0]
        found = jnp.where(mine & (count == slot), group, found)
        count = count + jnp.where(mine, 1, 0)
    return found, count > slot


def call_gather_groups(owner, device, w_query, w_key, w_value, w_out, slots):
    features = w_query.shape[2]
    arrays = (w_query, w_key, w_value, w_out)
    joint = slots * (w_query.shape[1] + w_key.shape[1] + w_value.shape[1])
    outs = [(joint, features), (slots * w_out.shape[1], features)]
    return pl.pallas_call(
        gather_groups,
        grid_spec=pltpu.PrefetchScalarGridSpec(
            num_scalar_prefetch=2,
            grid=(1,),
            in_specs=[pl.BlockSpec(memory_space=pl.ANY)] * 4,
            out_specs=[out_full_spec(o) for o in outs],
            scratch_shapes=[pltpu.SemaphoreType.DMA((4 * slots,))],
        ),
        out_shape=[shape_of(o, bf16) for o in outs],
        name="gather_groups",
    )(owner, device, *in_hbm(*arrays))


def rotary_tables(length):
    position = np.arange(length, dtype=np.float64)[None, :]
    column = np.arange(HEAD // 2, dtype=np.float64)[:, None]
    angles = position * np.exp(column * (-2.0 * math.log(10000.0) / HEAD))
    return jnp.asarray(np.cos(angles), f32), jnp.asarray(np.sin(angles), f32)


def exchange(own):
    return lax.ppermute(own, "mp", [(0, 1), (1, 0)])


def stage_plans(bit_count):
    bits = list(range(bit_count))
    turned = [bits[:3], bits[1:3] + bits[:1], bits[2:3] + bits[:2]]
    return [[[bit] for bit in first + bits[3:]] for first in turned]


def shard_order(plan):
    bits = [bit for stage in plan for bit in stage]
    order = []
    for place in range(1 << len(bits)):
        shard = 0
        for rank, bit in enumerate(bits):
            if place >> (len(bits) - 1 - rank) & 1:
                shard |= 1 << bit
        order.append(shard)
    return order


def after(value, *others):
    return lax.optimization_barrier((value, others))[0]


def slices(arrays, index, pieces):
    parts = [lax.dynamic_slice_in_dim(array, index * pieces, pieces, 0) for array in arrays]
    if len(parts) == 1:
        return parts[0]
    return sum(part.astype(f32) for part in parts).astype(bf16)


class Stream:
    def __init__(self, kept, stages):
        self.kept, self.stages = kept, list(stages)

    @classmethod
    def started(cls, kept, sent, plan):
        stream = cls([[kept]], plan)
        stream.transfer(sent, stream.stages.pop(0)[0])
        return stream

    def transfer(self, sent, bit):
        size = lax.axis_size("dp")
        received = lax.ppermute(sent, "dp", [(i, i ^ (1 << bit)) for i in range(size)])
        if len(self.kept) > 1:
            self.kept = [[jnp.concatenate([terms[0] for terms in self.kept], axis=2)]]
        self.kept[0].append(received)
        self.sent = sent

    def hold(self, *others):
        self.kept = after(self.kept, *others)
        return self

    def send(self):
        bit = self.stages.pop(0)[0]
        mine = (lax.axis_index("dp") >> bit) & 1
        pieces = self.kept[0][0].shape[0] // 2
        sent = [slices(terms, 1 - mine, pieces) for terms in self.kept]
        self.kept = [[slices(terms, mine, pieces)] for terms in self.kept]
        self.transfer(sent[0] if len(sent) == 1 else jnp.concatenate(sent, axis=2), bit)
        return self.sent

    def total(self):
        (terms,) = self.kept
        return sum(term[0].astype(f32) for term in terms)


def joined(streams):
    return Stream([terms for stream in streams for terms in stream.kept], streams[0].stages)


def per_device(
    tokens_in,
    segment_ids,
    kv_owner,
    w_query,
    w_key,
    w_value,
    w_out,
    attn_gain,
    w_gate,
    w_up,
    w_down,
    ffn_gain,
    cotangent,
):
    features = tokens_in.shape[2]
    length = tokens_in.shape[1]
    group_cols = w_query.shape[2]
    heads = group_cols // HEAD
    slots = (kv_owner.shape[0] + lax.axis_size("mp") - 1) // lax.axis_size("mp")
    size = lax.axis_size("dp")
    rows = features // size

    device = lax.axis_index("mp").astype(jnp.int32)[None]
    wqkv, wout = call_gather_groups(
        kv_owner, device, *(jnp.swapaxes(w, 1, 2) for w in (w_query, w_key, w_value)), w_out, slots
    )
    w_down = w_down.T
    segments = segment_ids[0]
    cosine, sine = rotary_tables(length)
    gain_one, gain_two = (
        jnp.broadcast_to(gain.astype(f32)[:, None], (features, LANES)) for gain in (attn_gain, ffn_gain)
    )

    parts = (tokens_in[0].T,)
    saved = []
    for _ in range(REPEAT):
        outs = list(call_attention_forward(segments, parts, gain_one, wqkv, wout, cosine, sine, slots, heads))
        hidden = outs.pop(0) if len(parts) == 3 else parts[0]
        normed, inverse, query, key, turned_key, value, attended, partial = outs
        middle, normed_two, inverse_two, gate, lift, inner, partial_two = call_ffn_forward(
            hidden, partial, exchange(partial), gain_two, w_gate, w_up, w_down
        )
        parts = (middle, partial_two, exchange(partial_two))
        saved.append((
            normed, inverse, query, key, turned_key, value, attended, normed_two, inverse_two, gate, lift, inner,
        ))

    plans = stage_plans(size.bit_length() - 1)
    orders = [shard_order(plan) for plan in plans]
    bits = jnp.stack([(lax.axis_index("dp") >> plan[0][0]) & 1 for plan in plans]).astype(jnp.int32)
    joint = ()
    grad = cotangent[0].T
    for r in reversed(range(REPEAT)):
        (normed, inverse, query, key, turned_key, value, attended,
         normed_two, inverse_two, gate, lift, inner) = saved[r]
        last = r == 0
        outs = list(call_ffn_backward(grad, joint, gate, lift, w_gate, w_up, w_down))
        if joint:
            grad = outs.pop(0)
        ffn_grad = grad
        grad_gate, grad_lift, partial = outs
        other = exchange(partial)
        if not last:
            parts = after(parts, partial)
            tokens_out = (parts[0] + (parts[1].astype(f32) + parts[2].astype(f32))).astype(bf16)
            grad = after(grad, tokens_out)
        else:
            payloads = call_ffn_weight_grad(
                bits, (above["normed_two"], normed_two), (above["ffn_grad"], ffn_grad),
                ((above["grad_gate"], grad_gate), (above["grad_lift"], grad_lift), (above["inner"], inner)),
                orders,
            )
            track_a, track_b, down = (
                Stream.started(*payload, plan) for payload, plan in zip(payloads, plans)
            )
            partial = after(partial, payloads)
        grad, projected, partial_two = call_attention_backward(
            segments, grad, partial, other, normed_two, inverse_two, gain_two, wout, wqkv, attended, query,
            key, turned_key, value, cosine, sine,
        )
        other_two = exchange(partial_two)
        if not last:
            above = dict(
                ffn_grad=ffn_grad, inner=inner, normed_two=normed_two, grad_lift=grad_lift,
                grad_gate=grad_gate, attention=(normed, projected, grad, attended),
            )
        joint = (normed, inverse, partial_two, other_two, gain_one)
    ffn = (track_a, track_b, down)
    sent = [stream.hold(projected).send() for stream in ffn]
    payloads = call_attention_weight_grad(
        bits, above["attention"], (normed, after(projected, sent), grad, attended), orders
    )
    tracks = [Stream.started(*payload, plan) for payload, plan in zip(payloads, plans)]
    for stream in ffn:
        stream.hold(payloads, other_two)
    sent = [stream.send() for stream in (track_a, track_b)]
    grad_in = call_block_grad(after(grad, sent, payloads), *joint, f32)
    both = joined([stream.hold(grad_in) for stream in (track_a, track_b)])
    sent = [both.send(), down.hold(grad_in).send()]
    sent = [stream.hold(sent).send() for stream in tracks]
    sent = [down.hold(sent).send()]
    while len(tracks[0].stages) > 1:
        sent = [stream.hold(sent).send() for stream in tracks]
    attn = joined([stream.hold(sent) for stream in tracks])
    pending = [both, down, attn]
    while any(stream.stages for stream in pending):
        for stream in pending:
            if stream.stages:
                stream.send()
    gate_total, up_total = jnp.split(both.total(), 2, axis=1)
    down_total = down.total()
    attn_total = attn.total()[:rows]

    start = lax.axis_index("dp") * rows

    def my_rows(weights):
        return lax.dynamic_slice_in_dim(weights, start, rows, 0).astype(f32)

    gate_total, up_total, down_total = (total[:rows] for total in (gate_total, up_total, down_total))
    wqkv = after(wqkv, grad_in)
    chosen = (jnp.arange(rows)[:, None] + start == jnp.arange(features)[None, :]).astype(bf16)
    wqkv_rows = matmul(chosen, wqkv, NT)
    joint_cols = wqkv.shape[0]
    gains = jnp.stack([
        jnp.sum(attn_total[:, :joint_cols] * wqkv_rows, axis=1),
        jnp.sum(gate_total * my_rows(w_gate) + up_total * my_rows(w_up), axis=1),
    ])
    gains = gains + exchange(gains)
    gains = gains / lax.dynamic_slice_in_dim(jnp.stack([attn_gain, ffn_gain]), start, rows, 1).astype(f32)

    ends = [group_cols, group_cols + HEAD]
    by_slot = jnp.moveaxis(attn_total[:, :joint_cols].reshape(rows, slots, -1), 1, 0)
    return (
        tokens_out.T[None],
        grad_in.T[None],
        by_slot[:, :, : ends[0]],
        by_slot[:, :, ends[0] : ends[1]],
        by_slot[:, :, ends[1] :],
        attn_total[:, joint_cols:].T.reshape(slots, group_cols, rows),
        gate_total,
        up_total,
        down_total.T,
        gains[0],
        gains[1],
    )


def solution(mesh):
    in_specs = (
        P("dp", None, None),
        P("dp", None),
        P(),
        P(),
        P(),
        P(),
        P(),
        P(),
        P(None, "mp"),
        P(None, "mp"),
        P("mp", None),
        P(),
        P("dp", None, None),
    )
    out_specs = (
        P("dp", None, None),
        P("dp", None, None),
        P("mp", "dp", None),
        P("mp", "dp", None),
        P("mp", "dp", None),
        P("mp", None, "dp"),
        P("dp", "mp"),
        P("dp", "mp"),
        P("mp", "dp"),
        P("dp"),
        P("dp"),
    )
    return jax.shard_map(
        per_device, mesh=mesh, in_specs=in_specs, out_specs=out_specs, check_vma=False
    )
```

profile of v0, /device:TPU:0, one launch (start us, length us, event | category | flops | bytes accessed | tf_op | source)
XLA Modules:
  0.0 299.1 jit_solution(11952891136410828670)
XLA Ops:
  0.7 4.1 %gather_groups.1 = (bf16[960,960]{1,0:T(8,128)(2,1)}, bf16[576,960]{1,0:T(8,128)(2,1)}) custom-call(s32[5]{0:T(128)} %owner.1, s32[1]{0:T(128)} %bitcast.4.device, bf16[5,192,960]{2,1,0:T(8,128)(2,1)} %bitcast.53, bf16[5,64,960]{2,1,0:T(8,128)(2,1)} %bitcast.54, bf16[5,64,960]{2,1,0:T(8,128)(2,1)} %bitcast.55, bf16[5,192,960]{2,1,0:T(8,128)(2,1)} %refs_3_.2), custom_call_target="tpu_custom_call" | custom-call | tf_op jit(solution)/shard_map/gather_groups/pallas_call | solution.py:700
  7.9 14.2 %attention_forward.2 = (bf16[960,1024]{1,0:T(8,128)(2,1)}, f32[1,1024]{1,0:T(1,128)}, bf16[4,3,128,768]{3,2,1,0:T(8,128)(2,1)}, bf16[1024,384]{1,0:T(8,128)(2,1)...) custom-call(s32[1024]{0:T(1024)S(1)} %bitcast.45, ...), custom_call_target="tpu_custom_call" | custom-call | flops 15019898880 | bytes 1966080 | tf_op jit(solution)/shard_map/attention_forward/pallas_call | solution.py:251
  22.9 3.6 %collective-permute-done.other_ref = bf16[960,1024]{1,0:T(8,128)(2,1)S(1)} collective-permute-done((bf16[960,1024]{1,0:T(8,128)(2,1)S(1)}, bf16[960,1024]{1,0:T(8,128)(2,1)S(1)}, u32[]{:S(2)}, u32[]{:S(2)}) %collective-permute-start) | collective-permute-done | bytes 1966112 | tf_op jit(solution)/shard_map/ppermute | solution.py:722
  26.7 13.2 %ffn_forward.2 = (f32[960,1024]{1,0:T(8,128)}, bf16[960,1024]{1,0:T(8,128)(2,1)}, f32[1,1024]{1,0:T(1,128)}, bf16[2,1280,512]{2,1,0:T(8,128)(2,1)}, bf16[2,1280,...) custom-call(bf16[960,1024]{1,0:T(8,128)(2,1)} %bitcast.61, ...), custom_call_target="tpu_custom_call" | custom-call | flops 7549747200 | bytes 1966080 | tf_op jit(solution)/shard_map/ffn_forward/pallas_call | solution.py:292
  40.3 3.6 %collective-permute-done.1.refs_2_ = bf16[960,1024]{1,0:T(8,128)(2,1)S(1)} collective-permute-done((bf16[960,1024]{1,0:T(8,128)(2,1)S(1)}, bf16[960,1024]{1,0:T(8,128)(2,1)S(1)}, u32[]{:S(2)}, u32[]{:S(2)}) %collective-permute-start.1) | collective-permute-done | bytes 1966112 | tf_op jit(solution)/shard_map/ppermute | solution.py:722
  43.9 15.7 %attention_forward.3 = (f32[960,1024]{1,0:T(8,128)}, bf16[960,1024]{1,0:T(8,128)(2,1)}, f32[1,1024]{1,0:T(1,128)}, bf16[4,3,128,768]{3,2,1,0:T(8,128)(2,1)}, bf1...) custom-call(s32[1024]{0:T(1024)S(1)} %bitcast.46, ...), custom_call_target="tpu_custom_call" | custom-call | flops 15019898880 | bytes 7864320 | tf_op jit(solution)/shard_map/attention_forward/pallas_call | solution.py:251
  60.0 3.6 %collective-permute-done.2.other_ref = bf16[960,1024]{1,0:T(8,128)(2,1)S(1)} collective-permute-done((bf16[960,1024]{1,0:T(8,128)(2,1)S(1)}, bf16[960,1024]{1,0:T(8,128)(2,1)S(1)}, u32[]{:S(2)}, u32[]{:S(2)}) %collective-permute-start.2) | collective-permute-done | bytes 1966112 | tf_op jit(solution)/shard_map/ppermute | solution.py:722
  63.6 13.1 %ffn_forward.3 = (f32[960,1024]{1,0:T(8,128)}, bf16[960,1024]{1,0:T(8,128)(2,1)}, f32[1,1024]{1,0:T(1,128)}, bf16[2,1280,512]{2,1,0:T(8,128)(2,1)}, bf16[2,1280,...) custom-call(f32[960,1024]{1,0:T(8,128)} %get-tuple-element.120.hidden_ref, ...), custom_call_target="tpu_custom_call" | custom-call | flops 7549747200 | bytes 3932160 | tf_op jit(solution)/shard_map/ffn_forward/pallas_call | solution.py:292
  77.1 22.2 %ffn_backward.2 = (bf16[2,1280,512]{2,1,0:T(8,128)(2,1)}, bf16[2,1280,512]{2,1,0:T(8,128)(2,1)}, bf16[960,1024]{1,0:T(8,128)(2,1)S(1)}) custom-call(bf16[960,1024]{1,0:T(8,128)(2,1)} %bitcast.62, bf16[2,1280,512]{2,1,0:T(8,128)(2,1)} %get-tuple-element.124.refs_0_, bf16[2,1280,512]{2,1,0:T(8,128)(2,1)} %get-tuple-element.125.refs_1_, ...), custom_call_target="tpu_custom_call" | custom-call | flops 7549747200 | bytes 1966080 | tf_op jit(solution)/shard_map/ffn_backward/pallas_call | solution.py:345
  103.3 21.6 %attention_backward.2 = (bf16[960,1024]{1,0:T(8,128)(2,1)}, bf16[960,1024]{1,0:T(8,128)(2,1)}, bf16[960,1024]{1,0:T(8,128)(2,1)S(1)}) custom-call(s32[1024]{0:T(1024)S(1)} %bitcast.47, bf16[960,1024]{1,0:T(8,128)(2,1)} %bitcast.63, bf16[960,1024]{1,0:T(8,128)(2,1)S(1)} %get-tuple-element.126.own_ref, bf16[960,1024]{1,0:T(8,128)(2,1)S(1)} %collective-permute-done.4.other_ref, ...), custom_call_target="tpu_custom_call" | custom-call | flops 27019898880 | bytes 1966080 | tf_op jit(solution)/shard_map/attention_backward/pallas_call | solution.py:442
  125.2 3.7 %collective-permute-done.5.refs_3_ = bf16[960,1024]{1,0:T(8,128)(2,1)S(1)} collective-permute-done((bf16[960,1024]{1,0:T(8,128)(2,1)S(1)}, bf16[960,1024]{1,0:T(8,128)(2,1)S(1)}, u32[]{:S(2)}, u32[]{:S(2)}) %collective-permute-start.5) | collective-permute-done | bytes 1966112 | tf_op jit(solution)/shard_map/ppermute | solution.py:722
  128.9 15.7 %ffn_backward.3 = (bf16[960,1024]{1,0:T(8,128)(2,1)}, bf16[2,1280,512]{2,1,0:T(8,128)(2,1)}, bf16[2,1280,512]{2,1,0:T(8,128)(2,1)}, bf16[960,1024]{1,0:T(8,128)(2,1)}) custom-call(bf16[960,1024]{1,0:T(8,128)(2,1)} %get-tuple-element.138.grad_ref.refs_4_, bf16[960,1024]{1,0:T(8,128)(2,1)} %get-tuple-element.139.refs_0_, f32[1,1024]{1,0:T(1,128)S(1)} %copy-done.18, ...), custom_call_target="tpu_custom_call" | custom-call | flops 7549747200 | bytes 1966080 | tf_op jit(solution)/shard_map/ffn_backward/pallas_call | solution.py:345
  145.0 24.3 %ffn_weight_grad.1 = (bf16[8,64,1280]{2,1,0:T(8,128)(2,1)}, bf16[8,64,1280]{2,1,0:T(8,128)(2,1)}, bf16[8,64,1280]{2,1,0:T(8,128)(2,1)}, bf16[8,64,1280]{2,1,0:T(...) custom-call(s32[3]{0:T(128)S(1)} %pad_add_fusion.bits, ...), custom_call_target="tpu_custom_call" | custom-call | flops 15099494400 | bytes 23592960 | tf_op jit(solution)/shard_map/ffn_weight_grad/pallas_call | solution.py:568
  171.8 7.1 %collective-permute-start.10 = (bf16[8,64,1280]{2,1,0:T(8,128)(2,1)}, bf16[8,64,1280]{2,1,0:T(8,128)(2,1)}, u32[]{:S(2)}, u32[]{:S(2)}) collective-permute-start(bf16[8,64,1280]{2,1,0:T(8,128)(2,1)} %get-tuple-element.158), channel_id=1, source_target_pairs={{0,8},{2,10},{4,12},{6,14},{8,0},{10,2},{12,4},{14,6},{16,24},{18,... | collective-permute-start | bytes 3932168 | tf_op jit(solution)/shard_map/ppermute | solution.py:766
  180.5 22.0 %attention_backward.3 = (bf16[960,1024]{1,0:T(8,128)(2,1)}, bf16[960,1024]{1,0:T(8,128)(2,1)}, bf16[960,1024]{1,0:T(8,128)(2,1)}) custom-call(s32[1024]{0:T(1024)S(1)} %bitcast.48, bf16[960,1024]{1,0:T(8,128)(2,1)} %get-tuple-element.144.refs_7_.grad_ref, bf16[960,1024]{1,0:T(8,128)(2,1)} %get-tuple-element.159.own_ref, ...), custom_call_target="tpu_custom_call" | custom-call | flops 27019898880 | bytes 1966080 | tf_op jit(solution)/shard_map/attention_backward/pallas_call | solution.py:442
  202.5 5.7 %collective-permute-done.10 = bf16[8,64,1280]{2,1,0:T(8,128)(2,1)} collective-permute-done((bf16[8,64,1280]{2,1,0:T(8,128)(2,1)}, bf16[8,64,1280]{2,1,0:T(8,128)(2,1)}, u32[]{:S(2)}, u32[]{:S(2)}) %collective-permute-start.10) | collective-permute-done | bytes 1310752 | tf_op jit(solution)/shard_map/ppermute | solution.py:766
  209.7 4.1 %add_convert_fusion.1 = (bf16[4,64,1280]{2,1,0:T(8,128)(2,1)S(1)}, bf16[4,64,1280]{2,1,0:T(8,128)(2,1)}, bf16[4,64,1280]{2,1,0:T(8,128)(2,1)}, bf16[4,64,1280]{2,1,0:T(8,128)(2,1)}) fusion(bf16[8,64,1280]{2,1,0:T(8,128)(2,1)} %collective-permute-done.10, s32[]{:T(128)S(6)} %select_n.40, bf16[8,64,1280]{2,1,0:T(8,128)(2,1)} %get-tuple-element.174, ...), kind=kLoop, calls=%fused_computation.1 | loop fusion | flops 5242880 | bytes 7864336 | tf_op jit(solution)/shard_map/convert_element_type | solution.py:751
  214.1 2.7 add_convert_fusion.5
  218.9 14.6 %attention_weight_grad.1 = (bf16[8,64,512]{2,1,0:T(8,128)(2,1)}, bf16[8,64,512]{2,1,0:T(8,128)(2,1)}, bf16[8,64,512]{2,1,0:T(8,128)(2,1)}, bf16[8,64,512]{2,1,0:...) custom-call(s32[3]{0:T(128)S(1)} %pad_add_fusion.bits, ...), custom_call_target="tpu_custom_call" | custom-call | flops 6039797760 | bytes 14155776 | tf_op jit(solution)/shard_map/attention_weight_grad/pallas_call | solution.py:568
  243.2 6.1 %block_grad.1 = f32[960,1024]{1,0:T(8,128)} custom-call(bf16[960,1024]{1,0:T(8,128)(2,1)} %get-tuple-element.188.refs_5_.grad_ref, bf16[960,1024]{1,0:T(8,128)(2,1)} %get-tuple-element.170.refs_1_.normed_ref, f32[1,1024]{1,0:T(1,128)S(1)} %copy-done.4, bf16[960,1024]{1,0:T(8,128)(2,1)} %get-tuple-element.183.own_ref, ...), custom_call_target="tpu_custom_call" | custom-call | bytes 7864320 | tf_op jit(solution)/shard_map/block_grad/pallas_call | solution.py:649
  254.4 3.7 %collective-permute-done.13 = bf16[8,64,512]{2,1,0:T(8,128)(2,1)S(1)} collective-permute-done((bf16[8,64,512]{2,1,0:T(8,128)(2,1)}, bf16[8,64,512]{2,1,0:T(8,128)(2,1)S(1)}, u32[]{:S(2)}, u32[]{:S(2)}) %collective-permute-start.13) | collective-permute-done | bytes 524320 | tf_op jit(solution)/shard_map/ppermute | solution.py:766
  267.2 7.0 %collective-permute-done.28 = bf16[1,64,1280]{2,1,0:T(8,128)(2,1)S(1)} collective-permute-done((bf16[1,64,1280]{2,1,0:T(8,128)(2,1)}, bf16[1,64,1280]{2,1,0:T(8,128)(2,1)S(1)}, u32[]{:S(2)}, u32[]{:S(2)}) %collective-permute-start.28) | collective-permute-done | bytes 163872 | tf_op jit(solution)/shard_map/ppermute | solution.py:766
  279.6 4.3 %collective-permute-done.27 = bf16[1,64,2560]{2,1,0:T(8,128)(2,1)S(1)} collective-permute-done((bf16[1,64,2560]{2,1,0:T(8,128)(2,1)}, bf16[1,64,2560]{2,1,0:T(8,128)(2,1)S(1)}, u32[]{:S(2)}, u32[]{:S(2)}) %collective-permute-start.27) | collective-permute-done | bytes 327712 | tf_op jit(solution)/shard_map/ppermute | solution.py:766
  288.4 5.6 %collective-permute-done.26 = bf16[1,64,1536]{2,1,0:T(8,128)(2,1)S(1)} collective-permute-done((bf16[1,64,1536]{2,1,0:T(8,128)(2,1)S(1)}, bf16[1,64,1536]{2,1,0:T(8,128)(2,1)S(1)}, u32[]{:S(2)}, u32[]{:S(2)}) %collective-permute-start.26) | collective-permute-done | bytes 196640 | tf_op jit(solution)/shard_map/ppermute | solution.py:766
  (162 shorter events, 56.1 us)
Async XLA Ops:
  76.7 22.9 %collective-permute-start.3 = (bf16[960,1024]{1,0:T(8,128)(2,1)S(1)}, bf16[960,1024]{1,0:T(8,128)(2,1)S(1)}, u32[]{:S(2)}, u32[]{:S(2)}) collective-permute-start(bf16[960,1024]{1,0:T(8,128)(2,1)S(1)} %get-tuple-element.128), channel_id=1, source_target_pairs={{0,1},{1,0},{2,3},{3,2},{4,5},{5,4},{6,7},{7,6},{8,9},{9,8},{10,11... | collective-permute-start | bytes 5898248 | tf_op jit(solution)/shard_map/ppermute | solution.py:722
  144.6 35.8 %collective-permute-start.6 = (bf16[960,1024]{1,0:T(8,128)(2,1)}, bf16[960,1024]{1,0:T(8,128)(2,1)}, u32[]{:S(2)}, u32[]{:S(2)}) collective-permute-start(bf16[960,1024]{1,0:T(8,128)(2,1)} %get-tuple-element.159.own_ref), channel_id=1, source_target_pairs={{0,1},{1,0},{2,3},{3,2},{4,5},{5,4},{6,7},{7,6},{8,9},{9,8},{10,11... | collective-permute-start | bytes 5898248 | tf_op jit(solution)/shard_map/ppermute | solution.py:722
  169.4 33.1 %collective-permute-start.9 = (bf16[8,64,1280]{2,1,0:T(8,128)(2,1)}, bf16[8,64,1280]{2,1,0:T(8,128)(2,1)}, u32[]{:S(2)}, u32[]{:S(2)}) collective-permute-start(bf16[8,64,1280]{2,1,0:T(8,128)(2,1)} %get-tuple-element.156), channel_id=1, source_target_pairs={{0,4},{2,6},{4,0},{6,2},{8,12},{10,14},{12,8},{14,10},{16,20},{18,... | collective-permute-start | bytes 3932168 | tf_op jit(solution)/shard_map/ppermute | solution.py:766
  171.8 36.4 %collective-permute-start.10 = (bf16[8,64,1280]{2,1,0:T(8,128)(2,1)}, bf16[8,64,1280]{2,1,0:T(8,128)(2,1)}, u32[]{:S(2)}, u32[]{:S(2)}) collective-permute-start(bf16[8,64,1280]{2,1,0:T(8,128)(2,1)} %get-tuple-element.158), channel_id=1, source_target_pairs={{0,8},{2,10},{4,12},{6,14},{8,0},{10,2},{12,4},{14,6},{16,24},{18,... | collective-permute-start | bytes 3932168 | tf_op jit(solution)/shard_map/ppermute | solution.py:766
  178.9 30.7 %collective-permute-start.7 = (bf16[8,64,1280]{2,1,0:T(8,128)(2,1)}, bf16[8,64,1280]{2,1,0:T(8,128)(2,1)}, u32[]{:S(2)}, u32[]{:S(2)}) collective-permute-start(bf16[8,64,1280]{2,1,0:T(8,128)(2,1)} %get-tuple-element.154), channel_id=1, source_target_pairs={{0,2},{2,0},{4,6},{6,4},{8,10},{10,8},{12,14},{14,12},{16,18},{18,... | collective-permute-start | bytes 3932168 | tf_op jit(solution)/shard_map/ppermute | solution.py:766
  202.4 31.1 %collective-permute-start.11 = (bf16[960,1024]{1,0:T(8,128)(2,1)}, bf16[960,1024]{1,0:T(8,128)(2,1)}, u32[]{:S(2)}, u32[]{:S(2)}) collective-permute-start(bf16[960,1024]{1,0:T(8,128)(2,1)} %get-tuple-element.183.own_ref), channel_id=1, source_target_pairs={{0,1},{1,0},{2,3},{3,2},{4,5},{5,4},{6,7},{7,6},{8,9},{9,8},{10,11... | collective-permute-start | bytes 5898248 | tf_op jit(solution)/shard_map/ppermute | solution.py:722
  213.8 19.7 %collective-permute-start.12 = (bf16[4,64,1280]{2,1,0:T(8,128)(2,1)}, bf16[4,64,1280]{2,1,0:T(8,128)(2,1)}, u32[]{:S(2)}, u32[]{:S(2)}) collective-permute-start(bf16[4,64,1280]{2,1,0:T(8,128)(2,1)} %get-tuple-element.282), channel_id=1, source_target_pairs={{0,8},{2,10},{4,12},{6,14},{8,0},{10,2},{12,4},{14,6},{16,24},{18,... | collective-permute-start | bytes 1966088 | tf_op jit(solution)/shard_map/ppermute | solution.py:766
  216.8 16.7 %collective-permute-start.8 = (bf16[4,64,1280]{2,1,0:T(8,128)(2,1)}, bf16[4,64,1280]{2,1,0:T(8,128)(2,1)}, u32[]{:S(2)}, u32[]{:S(2)}) collective-permute-start(bf16[4,64,1280]{2,1,0:T(8,128)(2,1)} %get-tuple-element.248), channel_id=1, source_target_pairs={{0,4},{2,6},{4,0},{6,2},{8,12},{10,14},{12,8},{14,10},{16,20},{18,... | collective-permute-start | bytes 1966088 | tf_op jit(solution)/shard_map/ppermute | solution.py:766
  217.4 25.5 %collective-permute-start.16 = (bf16[4,64,1280]{2,1,0:T(8,128)(2,1)}, bf16[4,64,1280]{2,1,0:T(8,128)(2,1)}, u32[]{:S(2)}, u32[]{:S(2)}) collective-permute-start(bf16[4,64,1280]{2,1,0:T(8,128)(2,1)} %get-tuple-element.245), channel_id=1, source_target_pairs={{0,2},{2,0},{4,6},{6,4},{8,10},{10,8},{12,14},{14,12},{16,18},{18,... | collective-permute-start | bytes 1966088 | tf_op jit(solution)/shard_map/ppermute | solution.py:766
  235.7 15.1 %collective-permute-start.14 = (bf16[2,64,1280]{2,1,0:T(8,128)(2,1)}, bf16[2,64,1280]{2,1,0:T(8,128)(2,1)}, u32[]{:S(2)}, u32[]{:S(2)}) collective-permute-start(bf16[2,64,1280]{2,1,0:T(8,128)(2,1)} %get-tuple-element.253), channel_id=1, source_target_pairs={{0,8},{2,10},{4,12},{6,14},{8,0},{10,2},{12,4},{14,6},{16,24},{18,... | collective-permute-start | bytes 983048 | tf_op jit(solution)/shard_map/ppermute | solution.py:766
  239.3 12.1 %collective-permute-start.15 = (bf16[2,64,1280]{2,1,0:T(8,128)(2,1)}, bf16[2,64,1280]{2,1,0:T(8,128)(2,1)}, u32[]{:S(2)}, u32[]{:S(2)}) collective-permute-start(bf16[2,64,1280]{2,1,0:T(8,128)(2,1)} %get-tuple-element.255), channel_id=1, source_target_pairs={{0,2},{2,0},{4,6},{6,4},{8,10},{10,8},{12,14},{14,12},{16,18},{18,... | collective-permute-start | bytes 983048 | tf_op jit(solution)/shard_map/ppermute | solution.py:766
  239.9 14.5 %collective-permute-start.19 = (bf16[8,64,512]{2,1,0:T(8,128)(2,1)}, bf16[8,64,512]{2,1,0:T(8,128)(2,1)S(1)}, u32[]{:S(2)}, u32[]{:S(2)}) collective-permute-start(bf16[8,64,512]{2,1,0:T(8,128)(2,1)} %get-tuple-element.180), channel_id=1, source_target_pairs={{0,4},{2,6},{4,0},{6,2},{8,12},{10,14},{12,8},{14,10},{16,20},{18,... | collective-permute-start | bytes 1572872 | tf_op jit(solution)/shard_map/ppermute | solution.py:766
  241.4 16.8 %collective-permute-start.13 = (bf16[8,64,512]{2,1,0:T(8,128)(2,1)}, bf16[8,64,512]{2,1,0:T(8,128)(2,1)S(1)}, u32[]{:S(2)}, u32[]{:S(2)}) collective-permute-start(bf16[8,64,512]{2,1,0:T(8,128)(2,1)} %get-tuple-element.178), channel_id=1, source_target_pairs={{0,2},{2,0},{4,6},{6,4},{8,10},{10,8},{12,14},{14,12},{16,18},{18,... | collective-permute-start | bytes 1572872 | tf_op jit(solution)/shard_map/ppermute | solution.py:766
  242.9 15.2 %collective-permute-start.20 = (bf16[8,64,512]{2,1,0:T(8,128)(2,1)}, bf16[8,64,512]{2,1,0:T(8,128)(2,1)S(1)}, u32[]{:S(2)}, u32[]{:S(2)}) collective-permute-start(bf16[8,64,512]{2,1,0:T(8,128)(2,1)} %get-tuple-element.182), channel_id=1, source_target_pairs={{0,8},{2,10},{4,12},{6,14},{8,0},{10,2},{12,4},{14,6},{16,24},{18,... | collective-permute-start | bytes 1572872 | tf_op jit(solution)/shard_map/ppermute | solution.py:766
  250.7 10.0 %collective-permute-start.18 = (bf16[2,64,1280]{2,1,0:T(8,128)(2,1)S(1)}, bf16[2,64,1280]{2,1,0:T(8,128)(2,1)S(1)}, u32[]{:S(2)}, u32[]{:S(2)}) collective-permute-start(bf16[2,64,1280]{2,1,0:T(8,128)(2,1)S(1)} %get-tuple-element.251), channel_id=1, source_target_pairs={{0,4},{2,6},{4,0},{6,2},{8,12},{10,14},{12,8},{14,10},{16,20},{18,... | collective-permute-start | bytes 983048 | tf_op jit(solution)/shard_map/ppermute | solution.py:766
  261.5 12.7 %collective-permute-start.28 = (bf16[1,64,1280]{2,1,0:T(8,128)(2,1)}, bf16[1,64,1280]{2,1,0:T(8,128)(2,1)S(1)}, u32[]{:S(2)}, u32[]{:S(2)}) collective-permute-start(bf16[1,64,1280]{2,1,0:T(8,128)(2,1)} %add_convert_fusion.22), channel_id=1, source_target_pairs={{0,16},{2,18},{4,20},{6,22},{8,24},{10,26},{12,28},{14,30},{16,0},... | collective-permute-start | bytes 491528 | tf_op jit(solution)/shard_map/ppermute | solution.py:766
  264.1 11.8 %collective-permute-start.22 = (bf16[4,64,512]{2,1,0:T(8,128)(2,1)}, bf16[4,64,512]{2,1,0:T(8,128)(2,1)S(1)}, u32[]{:S(2)}, u32[]{:S(2)}) collective-permute-start(bf16[4,64,512]{2,1,0:T(8,128)(2,1)} %get-tuple-element.257), channel_id=1, source_target_pairs={{0,8},{2,10},{4,12},{6,14},{8,0},{10,2},{12,4},{14,6},{16,24},{18,... | collective-permute-start | bytes 786440 | tf_op jit(solution)/shard_map/ppermute | solution.py:766
  265.0 11.0 %collective-permute-start.17 = (bf16[4,64,512]{2,1,0:T(8,128)(2,1)}, bf16[4,64,512]{2,1,0:T(8,128)(2,1)S(1)}, u32[]{:S(2)}, u32[]{:S(2)}) collective-permute-start(bf16[4,64,512]{2,1,0:T(8,128)(2,1)} %get-tuple-element.259), channel_id=1, source_target_pairs={{0,4},{2,6},{4,0},{6,2},{8,12},{10,14},{12,8},{14,10},{16,20},{18,... | collective-permute-start | bytes 786440 | tf_op jit(solution)/shard_map/ppermute | solution.py:766
  266.3 11.0 %collective-permute-start.23 = (bf16[4,64,512]{2,1,0:T(8,128)(2,1)}, bf16[4,64,512]{2,1,0:T(8,128)(2,1)S(1)}, u32[]{:S(2)}, u32[]{:S(2)}) collective-permute-start(bf16[4,64,512]{2,1,0:T(8,128)(2,1)} %get-tuple-element.260), channel_id=1, source_target_pairs={{0,2},{2,0},{4,6},{6,4},{8,10},{10,8},{12,14},{14,12},{16,18},{18,... | collective-permute-start | bytes 786440 | tf_op jit(solution)/shard_map/ppermute | solution.py:766
  266.9 17.0 %collective-permute-start.27 = (bf16[1,64,2560]{2,1,0:T(8,128)(2,1)}, bf16[1,64,2560]{2,1,0:T(8,128)(2,1)S(1)}, u32[]{:S(2)}, u32[]{:S(2)}) collective-permute-start(bf16[1,64,2560]{2,1,0:T(8,128)(2,1)} %pad_maximum_fusion), channel_id=1, source_target_pairs={{0,16},{2,18},{4,20},{6,22},{8,24},{10,26},{12,28},{14,30},{16,0},... | collective-permute-start | bytes 983048 | tf_op jit(solution)/shard_map/ppermute | solution.py:766
  276.1 8.3 %collective-permute-start.21 = (bf16[2,64,512]{2,1,0:T(8,128)(2,1)S(1)}, bf16[2,64,512]{2,1,0:T(8,128)(2,1)S(1)}, u32[]{:S(2)}, u32[]{:S(2)}) collective-permute-start(bf16[2,64,512]{2,1,0:T(8,128)(2,1)S(1)} %get-tuple-element.267), channel_id=1, source_target_pairs={{0,8},{2,10},{4,12},{6,14},{8,0},{10,2},{12,4},{14,6},{16,24},{18,... | collective-permute-start | bytes 393224 | tf_op jit(solution)/shard_map/ppermute | solution.py:766
  277.3 7.1 %collective-permute-start.24 = (bf16[2,64,512]{2,1,0:T(8,128)(2,1)S(1)}, bf16[2,64,512]{2,1,0:T(8,128)(2,1)S(1)}, u32[]{:S(2)}, u32[]{:S(2)}) collective-permute-start(bf16[2,64,512]{2,1,0:T(8,128)(2,1)S(1)} %get-tuple-element.269), channel_id=1, source_target_pairs={{0,2},{2,0},{4,6},{6,4},{8,10},{10,8},{12,14},{14,12},{16,18},{18,... | collective-permute-start | bytes 393224 | tf_op jit(solution)/shard_map/ppermute | solution.py:766
  278.0 6.4 %collective-permute-start.25 = (bf16[2,64,512]{2,1,0:T(8,128)(2,1)S(1)}, bf16[2,64,512]{2,1,0:T(8,128)(2,1)S(1)}, u32[]{:S(2)}, u32[]{:S(2)}) collective-permute-start(bf16[2,64,512]{2,1,0:T(8,128)(2,1)S(1)} %get-tuple-element.270), channel_id=1, source_target_pairs={{0,4},{2,6},{4,0},{6,2},{8,12},{10,14},{12,8},{14,10},{16,20},{18,... | collective-permute-start | bytes 393224 | tf_op jit(solution)/shard_map/ppermute | solution.py:766
  284.5 9.4 %collective-permute-start.26 = (bf16[1,64,1536]{2,1,0:T(8,128)(2,1)S(1)}, bf16[1,64,1536]{2,1,0:T(8,128)(2,1)S(1)}, u32[]{:S(2)}, u32[]{:S(2)}) collective-permute-start(bf16[1,64,1536]{2,1,0:T(8,128)(2,1)S(1)} %pad_maximum_fusion.1), channel_id=1, source_target_pairs={{0,16},{2,18},{4,20},{6,22},{8,24},{10,26},{12,28},{14,30},{16,0},... | collective-permute-start | bytes 589832 | tf_op jit(solution)/shard_map/ppermute | solution.py:766
  (41 other events, 476.5 us)
where the time goes:
time: 302 us; the launch traced here: 299 us
  Pallas kernels  187 us (62%)
  waiting for transfers between devices  44.1 us (15%)
  starting transfers between devices  33.4 us (11%)
  other arithmetic  25.4 us (8%)
  local copies, waits for them, and re-layouts  7.18 us (2%)
    pallas_call x2, Pallas kernels, call_attention_backward(): pl.pallas_call(functools.partial(attention_backward, slots, heads), grid_...  43.5 us
    pallas_call x2, Pallas kernels, call_weight_grad(): pl.pallas_call(functools.partial(kernel, orders, rows), grid_spec=pltpu.P...  38.9 us
    pallas_call x2, Pallas kernels, call_ffn_backward(): pl.pallas_call(functools.partial(ffn_backward, bool(joint)), grid=(length...  37.9 us
    ppermute x21, starting transfers between devices, transfer(): lax.ppermute(sent, 'dp', [(i, i ^ 1 << bit) for i in range(size)])  30.4 us
    pallas_call x2, Pallas kernels, call_attention_forward(): pl.pallas_call(functools.partial(attention_forward, joined, slots, heads)...  29.8 us
    ppermute x21, waiting for transfers between devices, transfer(): lax.ppermute(sent, 'dp', [(i, i ^ 1 << bit) for i in range(size)])  28.3 us
    pallas_call x2, Pallas kernels, call_ffn_forward(): pl.pallas_call(ffn_forward, grid=(length // FFN_BLOCK,), in_specs=[spec(f...  26.3 us
    convert_element_type x17, other arithmetic, slices(): return sum((part.astype(f32) for part in parts)).astype(bf16)  18.2 us
  transfers between devices with their start and end apart: 30, of which 12 were waited for; matrix products, arithmetic and copies ran while one was open for 9% of the time, Pallas kernels for 30%

commit v1 on v0

--- a/solution.py
+++ b/solution.py
@@ -744,51 +744,68 @@
     return lax.optimization_barrier((value, others))[0]
 
 
-def slices(arrays, index, pieces):
-    parts = [lax.dynamic_slice_in_dim(array, index * pieces, pieces, 0) for array in arrays]
-    if len(parts) == 1:
-        return parts[0]
-    return sum(part.astype(f32) for part in parts).astype(bf16)
-
-
 class Stream:
-    def __init__(self, kept, stages):
-        self.kept, self.stages = kept, list(stages)
+    def __init__(self, parts, widths, count, stages):
+        self.parts, self.widths, self.count, self.stages = parts, widths, count, list(stages)
 
     @classmethod
     def started(cls, kept, sent, plan):
-        stream = cls([[kept]], plan)
+        stream = cls([[(kept, 0, 0)]], [kept.shape[2]], kept.shape[0], plan)
         stream.transfer(sent, stream.stages.pop(0)[0])
         return stream
 
     def transfer(self, sent, bit):
         size = lax.axis_size("dp")
         received = lax.ppermute(sent, "dp", [(i, i ^ (1 << bit)) for i in range(size)])
-        if len(self.kept) > 1:
-            self.kept = [[jnp.concatenate([terms[0] for terms in self.kept], axis=2)]]
-        self.kept[0].append(received)
+        column = 0
+        for terms, width in zip(self.parts, self.widths):
+            terms.append((received, 0, column))
+            column += width
         self.sent = sent
 
     def hold(self, *others):
-        self.kept = after(self.kept, *others)
+        received = after(self.parts[0][-1][0], *others)
+        for terms in self.parts:
+            terms[-1] = (received, *terms[-1][1:])
         return self
 
-    def send(self):
+    def sums(self, first, count):
+        out = []
+        for terms, width in zip(self.parts, self.widths):
+            pieces = [
+                lax.dynamic_slice(array, (start + first, 0, column), (count, array.shape[1], width))
+                for array, start, column in terms
+            ]
+            out.append(sum(piece.astype(f32) for piece in pieces))
+        return out
+
+    def send(self, eager=False):
         bit = self.stages.pop(0)[0]
         mine = (lax.axis_index("dp") >> bit) & 1
-        pieces = self.kept[0][0].shape[0] // 2
-        sent = [slices(terms, 1 - mine, pieces) for terms in self.kept]
-        self.kept = [[slices(terms, mine, pieces)] for terms in self.kept]
+        self.count //= 2
+        sent = [piece.astype(bf16) for piece in self.sums((1 - mine) * self.count, self.count)]
+        if eager:
+            kept = self.sums(mine * self.count, self.count)
+            self.parts = [[(piece.astype(bf16), 0, 0)] for piece in kept]
+        else:
+            self.parts = [
+                [(array, start + mine * self.count, column) for array, start, column in terms]
+                for terms in self.parts
+            ]
         self.transfer(sent[0] if len(sent) == 1 else jnp.concatenate(sent, axis=2), bit)
         return self.sent
 
-    def total(self):
-        (terms,) = self.kept
-        return sum(term[0].astype(f32) for term in terms)
+    def totals(self):
+        return [piece[0] for piece in self.sums(0, 1)]
 
 
 def joined(streams):
-    return Stream([terms for stream in streams for terms in stream.kept], streams[0].stages)
+    return Stream(
+        [terms for stream in streams for terms in stream.parts],
+        [width for stream in streams for width in stream.widths],
+        streams[0].count,
+        streams[0].stages,
+    )
 
 
 def per_device(
@@ -890,20 +907,20 @@
     sent = [stream.send() for stream in (track_a, track_b)]
     grad_in = call_block_grad(after(grad, sent, payloads), *joint, f32)
     both = joined([stream.hold(grad_in) for stream in (track_a, track_b)])
-    sent = [both.send(), down.hold(grad_in).send()]
-    sent = [stream.hold(sent).send() for stream in tracks]
-    sent = [down.hold(sent).send()]
+    sent = [both.send(True), down.hold(grad_in).send(True)]
+    sent = [stream.hold(sent).send(True) for stream in tracks]
+    sent = [down.hold(sent).send(True)]
     while len(tracks[0].stages) > 1:
-        sent = [stream.hold(sent).send() for stream in tracks]
+        sent = [stream.hold(sent).send(True) for stream in tracks]
     attn = joined([stream.hold(sent) for stream in tracks])
     pending = [both, down, attn]
     while any(stream.stages for stream in pending):
         for stream in pending:
             if stream.stages:
-                stream.send()
-    gate_total, up_total = jnp.split(both.total(), 2, axis=1)
-    down_total = down.total()
-    attn_total = attn.total()[:rows]
+                stream.send(True)
+    gate_total, up_total = both.totals()
+    (down_total,) = down.totals()
+    attn_total = jnp.concatenate(attn.totals(), axis=1)[:rows]
 
     start = lax.axis_index("dp") * rows
 

time: 302 us -> 295 us (0.977)
  starting transfers between devices: 33.4 us -> 25.3 us
  Pallas kernels: 187 us -> 195 us
  other arithmetic: 25.4 us -> 19.2 us
    ppermute x21, starting transfers between devices: 30.4 us -> 22.2 us  [transfer(): lax.ppermute(sent, 'dp', [(i, i ^ 1 << bit) for i in range(size)])]
    pallas_call x2, Pallas kernels: 43.5 us -> 50 us  [call_attention_backward(): pl.pallas_call(functools.partial(attention_backward, slots, heads), grid_...]
    convert_element_type x17 -> x20, other arithmetic: 18.2 us -> 13.5 us  [the longest x10 8.42 us: send(): piece.astype(bf16)]
    unnamed x74 -> x64, local copies, waits for them, and re-layouts: 5.68 us -> 6.29 us
  transfers between devices with their start and end apart: 30 -> 30, of which waited for: 12 -> 14; matrix products, arithmetic and copies ran while one was open for 9% -> 8% of each run, Pallas kernels for 30% -> 32%
where the time goes in v1:
time: 295 us; the launch traced here: 292 us
  Pallas kernels  195 us (66%)
  waiting for transfers between devices  42 us (14%)
  starting transfers between devices  25.3 us (9%)
  other arithmetic  19.2 us (7%)
  local copies, waits for them, and re-layouts  7.69 us (3%)
    pallas_call x2, Pallas kernels, call_attention_backward(): pl.pallas_call(functools.partial(attention_backward, slots, heads), grid_...  50 us
    pallas_call x2, Pallas kernels, call_weight_grad(): pl.pallas_call(functools.partial(kernel, orders, rows), grid_spec=pltpu.P...  38.8 us
    pallas_call x2, Pallas kernels, call_ffn_backward(): pl.pallas_call(functools.partial(ffn_backward, bool(joint)), grid=(length...  37.9 us
    pallas_call x2, Pallas kernels, call_attention_forward(): pl.pallas_call(functools.partial(attention_forward, joined, slots, heads)...  32.2 us
    pallas_call x2, Pallas kernels, call_ffn_forward(): pl.pallas_call(ffn_forward, grid=(length // FFN_BLOCK,), in_specs=[spec(f...  26.2 us
    ppermute x21, waiting for transfers between devices, transfer(): lax.ppermute(sent, 'dp', [(i, i ^ 1 << bit) for i in range(size)])  26.2 us
    ppermute x21, starting transfers between devices, transfer(): lax.ppermute(sent, 'dp', [(i, i ^ 1 << bit) for i in range(size)])  22.2 us
    ppermute x9, waiting for transfers between devices, exchange(): return lax.ppermute(own, 'mp', [(0, 1), (1, 0)])  15.7 us
  transfers between devices with their start and end apart: 30, of which 14 were waited for; matrix products, arithmetic and copies ran while one was open for 8% of the time, Pallas kernels for 32%

profile of v1, /device:TPU:0, one launch (start us, length us, event | category | flops | bytes accessed | tf_op | source)
XLA Modules:
  0.0 291.9 jit_solution(3501472761007691941)
XLA Ops:
  0.7 4.1 %gather_groups.1 = (bf16[960,960]{1,0:T(8,128)(2,1)}, bf16[576,960]{1,0:T(8,128)(2,1)}) custom-call(s32[5]{0:T(128)} %owner.1, s32[1]{0:T(128)} %bitcast.4.device, bf16[5,192,960]{2,1,0:T(8,128)(2,1)} %bitcast.61, bf16[5,64,960]{2,1,0:T(8,128)(2,1)} %bitcast.62, bf16[5,64,960]{2,1,0:T(8,128)(2,1)} %bitcast.63, bf16[5,192,960]{2,1,0:T(8,128)(2,1)} %refs_3_.2), custom_call_target="tpu_custom_call" | custom-call | tf_op jit(solution)/shard_map/gather_groups/pallas_call | solution.py:700
  7.9 15.3 %attention_forward.2 = (bf16[960,1024]{1,0:T(8,128)(2,1)}, f32[1,1024]{1,0:T(1,128)}, bf16[4,3,128,768]{3,2,1,0:T(8,128)(2,1)}, bf16[1024,384]{1,0:T(8,128)(2,1)...) custom-call(s32[1024]{0:T(1024)S(1)} %bitcast.53, ...), custom_call_target="tpu_custom_call" | custom-call | flops 15019898880 | bytes 1966080 | tf_op jit(solution)/shard_map/attention_forward/pallas_call | solution.py:251
  24.0 3.6 %collective-permute-done.other_ref = bf16[960,1024]{1,0:T(8,128)(2,1)S(1)} collective-permute-done((bf16[960,1024]{1,0:T(8,128)(2,1)S(1)}, bf16[960,1024]{1,0:T(8,128)(2,1)S(1)}, u32[]{:S(2)}, u32[]{:S(2)}) %collective-permute-start) | collective-permute-done | bytes 1966112 | tf_op jit(solution)/shard_map/ppermute | solution.py:722
  27.8 13.2 %ffn_forward.2 = (f32[960,1024]{1,0:T(8,128)}, bf16[960,1024]{1,0:T(8,128)(2,1)}, f32[1,1024]{1,0:T(1,128)}, bf16[2,1280,512]{2,1,0:T(8,128)(2,1)}, bf16[2,1280,...) custom-call(bf16[960,1024]{1,0:T(8,128)(2,1)} %bitcast.69, ...), custom_call_target="tpu_custom_call" | custom-call | flops 7549747200 | bytes 1966080 | tf_op jit(solution)/shard_map/ffn_forward/pallas_call | solution.py:292
  41.4 3.6 %collective-permute-done.1.refs_2_ = bf16[960,1024]{1,0:T(8,128)(2,1)S(1)} collective-permute-done((bf16[960,1024]{1,0:T(8,128)(2,1)S(1)}, bf16[960,1024]{1,0:T(8,128)(2,1)S(1)}, u32[]{:S(2)}, u32[]{:S(2)}) %collective-permute-start.1) | collective-permute-done | bytes 1966112 | tf_op jit(solution)/shard_map/ppermute | solution.py:722
  45.0 16.8 %attention_forward.3 = (f32[960,1024]{1,0:T(8,128)}, bf16[960,1024]{1,0:T(8,128)(2,1)}, f32[1,1024]{1,0:T(1,128)}, bf16[4,3,128,768]{3,2,1,0:T(8,128)(2,1)}, bf1...) custom-call(s32[1024]{0:T(1024)S(1)} %bitcast.54, ...), custom_call_target="tpu_custom_call" | custom-call | flops 15019898880 | bytes 7864320 | tf_op jit(solution)/shard_map/attention_forward/pallas_call | solution.py:251
  62.2 3.6 %collective-permute-done.2.other_ref = bf16[960,1024]{1,0:T(8,128)(2,1)S(1)} collective-permute-done((bf16[960,1024]{1,0:T(8,128)(2,1)S(1)}, bf16[960,1024]{1,0:T(8,128)(2,1)S(1)}, u32[]{:S(2)}, u32[]{:S(2)}) %collective-permute-start.2) | collective-permute-done | bytes 1966112 | tf_op jit(solution)/shard_map/ppermute | solution.py:722
  65.8 13.1 %ffn_forward.3 = (f32[960,1024]{1,0:T(8,128)}, bf16[960,1024]{1,0:T(8,128)(2,1)}, f32[1,1024]{1,0:T(1,128)}, bf16[2,1280,512]{2,1,0:T(8,128)(2,1)}, bf16[2,1280,...) custom-call(f32[960,1024]{1,0:T(8,128)} %get-tuple-element.101.hidden_ref, ...), custom_call_target="tpu_custom_call" | custom-call | flops 7549747200 | bytes 3932160 | tf_op jit(solution)/shard_map/ffn_forward/pallas_call | solution.py:292
  79.3 22.2 %ffn_backward.2 = (bf16[2,1280,512]{2,1,0:T(8,128)(2,1)}, bf16[2,1280,512]{2,1,0:T(8,128)(2,1)}, bf16[960,1024]{1,0:T(8,128)(2,1)S(1)}) custom-call(bf16[960,1024]{1,0:T(8,128)(2,1)} %bitcast.70, bf16[2,1280,512]{2,1,0:T(8,128)(2,1)} %get-tuple-element.105.refs_0_, bf16[2,1280,512]{2,1,0:T(8,128)(2,1)} %get-tuple-element.106.refs_1_, ...), custom_call_target="tpu_custom_call" | custom-call | flops 7549747200 | bytes 1966080 | tf_op jit(solution)/shard_map/ffn_backward/pallas_call | solution.py:345
  101.8 2.4 add_convert_fusion
  105.5 24.8 %attention_backward.2 = (bf16[960,1024]{1,0:T(8,128)(2,1)}, bf16[960,1024]{1,0:T(8,128)(2,1)}, bf16[960,1024]{1,0:T(8,128)(2,1)S(1)}) custom-call(s32[1024]{0:T(1024)S(1)} %bitcast.55, bf16[960,1024]{1,0:T(8,128)(2,1)} %bitcast.71, bf16[960,1024]{1,0:T(8,128)(2,1)S(1)} %get-tuple-element.107.own_ref, bf16[960,1024]{1,0:T(8,128)(2,1)S(1)} %collective-permute-done.4.other_ref, ...), custom_call_target="tpu_custom_call" | custom-call | flops 27019898880 | bytes 1966080 | tf_op jit(solution)/shard_map/attention_backward/pallas_call | solution.py:442
  130.6 3.7 %collective-permute-done.5.refs_3_ = bf16[960,1024]{1,0:T(8,128)(2,1)S(1)} collective-permute-done((bf16[960,1024]{1,0:T(8,128)(2,1)S(1)}, bf16[960,1024]{1,0:T(8,128)(2,1)S(1)}, u32[]{:S(2)}, u32[]{:S(2)}) %collective-permute-start.5) | collective-permute-done | bytes 1966112 | tf_op jit(solution)/shard_map/ppermute | solution.py:722
  134.3 15.7 %ffn_backward.3 = (bf16[960,1024]{1,0:T(8,128)(2,1)}, bf16[2,1280,512]{2,1,0:T(8,128)(2,1)}, bf16[2,1280,512]{2,1,0:T(8,128)(2,1)}, bf16[960,1024]{1,0:T(8,128)(2,1)}) custom-call(bf16[960,1024]{1,0:T(8,128)(2,1)} %get-tuple-element.119.grad_ref.refs_4_, bf16[960,1024]{1,0:T(8,128)(2,1)} %get-tuple-element.120.refs_0_, f32[1,1024]{1,0:T(1,128)S(1)} %copy-done.18, ...), custom_call_target="tpu_custom_call" | custom-call | flops 7549747200 | bytes 1966080 | tf_op jit(solution)/shard_map/ffn_backward/pallas_call | solution.py:345
  150.5 24.3 %ffn_weight_grad.1 = (bf16[8,64,1280]{2,1,0:T(8,128)(2,1)}, bf16[8,64,1280]{2,1,0:T(8,128)(2,1)}, bf16[8,64,1280]{2,1,0:T(8,128)(2,1)}, bf16[8,64,1280]{2,1,0:T(...) custom-call(s32[3]{0:T(128)S(1)} %pad_add_fusion.bits, ...), custom_call_target="tpu_custom_call" | custom-call | flops 15099494400 | bytes 23592960 | tf_op jit(solution)/shard_map/ffn_weight_grad/pallas_call | solution.py:568
  174.8 2.5 collective-permute-start.10
  178.9 25.2 %attention_backward.3 = (bf16[960,1024]{1,0:T(8,128)(2,1)}, bf16[960,1024]{1,0:T(8,128)(2,1)}, bf16[960,1024]{1,0:T(8,128)(2,1)}) custom-call(s32[1024]{0:T(1024)S(1)} %bitcast.56, bf16[960,1024]{1,0:T(8,128)(2,1)} %get-tuple-element.125.refs_7_.grad_ref, bf16[960,1024]{1,0:T(8,128)(2,1)} %get-tuple-element.140.own_ref, ...), custom_call_target="tpu_custom_call" | custom-call | flops 27019898880 | bytes 1966080 | tf_op jit(solution)/shard_map/attention_backward/pallas_call | solution.py:442
  216.1 14.5 %attention_weight_grad.1 = (bf16[8,64,512]{2,1,0:T(8,128)(2,1)}, bf16[8,64,512]{2,1,0:T(8,128)(2,1)}, bf16[8,64,512]{2,1,0:T(8,128)(2,1)}, bf16[8,64,512]{2,1,0:...) custom-call(s32[3]{0:T(128)S(1)} %pad_add_fusion.bits, ...), custom_call_target="tpu_custom_call" | custom-call | flops 6039797760 | bytes 14155776 | tf_op jit(solution)/shard_map/attention_weight_grad/pallas_call | solution.py:568
  239.8 6.1 %block_grad.1 = f32[960,1024]{1,0:T(8,128)} custom-call(bf16[960,1024]{1,0:T(8,128)(2,1)} %get-tuple-element.164.refs_5_.grad_ref, bf16[960,1024]{1,0:T(8,128)(2,1)} %get-tuple-element.150.refs_1_.normed_ref, f32[1,1024]{1,0:T(1,128)S(1)} %copy-done.4, bf16[960,1024]{1,0:T(8,128)(2,1)} %get-tuple-element.161.own_ref, ...), custom_call_target="tpu_custom_call" | custom-call | bytes 7864320 | tf_op jit(solution)/shard_map/block_grad/pallas_call | solution.py:649
  247.9 3.2 %collective-permute-done.15 = bf16[2,64,1280]{2,1,0:T(8,128)(2,1)S(1)} collective-permute-done((bf16[2,64,1280]{2,1,0:T(8,128)(2,1)S(1)}, bf16[2,64,1280]{2,1,0:T(8,128)(2,1)S(1)}, u32[]{:S(2)}, u32[]{:S(2)}) %collective-permute-start.15) | collective-permute-done | bytes 327712 | tf_op jit(solution)/shard_map/ppermute | solution.py:759
  254.5 2.8 collective-permute-start.28
  261.1 4.0 %collective-permute-done.28 = bf16[1,64,1280]{2,1,0:T(8,128)(2,1)S(1)} collective-permute-done((bf16[1,64,1280]{2,1,0:T(8,128)(2,1)S(1)}, bf16[1,64,1280]{2,1,0:T(8,128)(2,1)S(1)}, u32[]{:S(2)}, u32[]{:S(2)}) %collective-permute-start.28) | collective-permute-done | bytes 163872 | tf_op jit(solution)/shard_map/ppermute | solution.py:759
  265.8 3.8 %collective-permute-done.22 = bf16[4,64,512]{2,1,0:T(8,128)(2,1)S(1)} collective-permute-done((bf16[4,64,512]{2,1,0:T(8,128)(2,1)S(1)}, bf16[4,64,512]{2,1,0:T(8,128)(2,1)S(1)}, u32[]{:S(2)}, u32[]{:S(2)}) %collective-permute-start.22) | collective-permute-done | bytes 262176 | tf_op jit(solution)/shard_map/ppermute | solution.py:759
  271.5 5.3 %collective-permute-done.27 = bf16[1,64,2560]{2,1,0:T(8,128)(2,1)S(1)} collective-permute-done((bf16[1,64,2560]{2,1,0:T(8,128)(2,1)S(1)}, bf16[1,64,2560]{2,1,0:T(8,128)(2,1)S(1)}, u32[]{:S(2)}, u32[]{:S(2)}) %collective-permute-start.27) | collective-permute-done | bytes 327712 | tf_op jit(solution)/shard_map/ppermute | solution.py:759
  280.8 5.9 %collective-permute-done.26 = bf16[1,64,1536]{2,1,0:T(8,128)(2,1)S(1)} collective-permute-done((bf16[1,64,1536]{2,1,0:T(8,128)(2,1)S(1)}, bf16[1,64,1536]{2,1,0:T(8,128)(2,1)S(1)}, u32[]{:S(2)}, u32[]{:S(2)}) %collective-permute-start.26) | collective-permute-done | bytes 196640 | tf_op jit(solution)/shard_map/ppermute | solution.py:759
  (155 shorter events, 50.8 us)
Async XLA Ops:
  78.9 22.9 %collective-permute-start.3 = (bf16[960,1024]{1,0:T(8,128)(2,1)S(1)}, bf16[960,1024]{1,0:T(8,128)(2,1)S(1)}, u32[]{:S(2)}, u32[]{:S(2)}) collective-permute-start(bf16[960,1024]{1,0:T(8,128)(2,1)S(1)} %get-tuple-element.109), channel_id=1, source_target_pairs={{0,1},{1,0},{2,3},{3,2},{4,5},{5,4},{6,7},{7,6},{8,9},{9,8},{10,11... | collective-permute-start | bytes 5898248 | tf_op jit(solution)/shard_map/ppermute | solution.py:722
  150.0 28.8 %collective-permute-start.6 = (bf16[960,1024]{1,0:T(8,128)(2,1)}, bf16[960,1024]{1,0:T(8,128)(2,1)}, u32[]{:S(2)}, u32[]{:S(2)}) collective-permute-start(bf16[960,1024]{1,0:T(8,128)(2,1)} %get-tuple-element.140.own_ref), channel_id=1, source_target_pairs={{0,1},{1,0},{2,3},{3,2},{4,5},{5,4},{6,7},{7,6},{8,9},{9,8},{10,11... | collective-permute-start | bytes 5898248 | tf_op jit(solution)/shard_map/ppermute | solution.py:722
  174.8 32.1 %collective-permute-start.10 = (bf16[8,64,1280]{2,1,0:T(8,128)(2,1)}, bf16[8,64,1280]{2,1,0:T(8,128)(2,1)}, u32[]{:S(2)}, u32[]{:S(2)}) collective-permute-start(bf16[8,64,1280]{2,1,0:T(8,128)(2,1)} %get-tuple-element.139), channel_id=1, source_target_pairs={{0,8},{2,10},{4,12},{6,14},{8,0},{10,2},{12,4},{14,6},{16,24},{18,... | collective-permute-start | bytes 3932168 | tf_op jit(solution)/shard_map/ppermute | solution.py:759
  177.3 31.0 %collective-permute-start.9 = (bf16[8,64,1280]{2,1,0:T(8,128)(2,1)}, bf16[8,64,1280]{2,1,0:T(8,128)(2,1)}, u32[]{:S(2)}, u32[]{:S(2)}) collective-permute-start(bf16[8,64,1280]{2,1,0:T(8,128)(2,1)} %get-tuple-element.137), channel_id=1, source_target_pairs={{0,4},{2,6},{4,0},{6,2},{8,12},{10,14},{12,8},{14,10},{16,20},{18,... | collective-permute-start | bytes 3932168 | tf_op jit(solution)/shard_map/ppermute | solution.py:759
  177.3 31.0 %collective-permute-start.7 = (bf16[8,64,1280]{2,1,0:T(8,128)(2,1)}, bf16[8,64,1280]{2,1,0:T(8,128)(2,1)}, u32[]{:S(2)}, u32[]{:S(2)}) collective-permute-start(bf16[8,64,1280]{2,1,0:T(8,128)(2,1)} %get-tuple-element.135), channel_id=1, source_target_pairs={{0,2},{2,0},{4,6},{6,4},{8,10},{10,8},{12,14},{14,12},{16,18},{18,... | collective-permute-start | bytes 3932168 | tf_op jit(solution)/shard_map/ppermute | solution.py:759
  204.1 28.5 %collective-permute-start.11 = (bf16[960,1024]{1,0:T(8,128)(2,1)}, bf16[960,1024]{1,0:T(8,128)(2,1)}, u32[]{:S(2)}, u32[]{:S(2)}) collective-permute-start(bf16[960,1024]{1,0:T(8,128)(2,1)} %get-tuple-element.161.own_ref), channel_id=1, source_target_pairs={{0,1},{1,0},{2,3},{3,2},{4,5},{5,4},{6,7},{7,6},{8,9},{9,8},{10,11... | collective-permute-start | bytes 5898248 | tf_op jit(solution)/shard_map/ppermute | solution.py:722
  209.7 22.5 %collective-permute-start.12 = (bf16[4,64,1280]{2,1,0:T(8,128)(2,1)S(1)}, bf16[4,64,1280]{2,1,0:T(8,128)(2,1)S(1)}, u32[]{:S(2)}, u32[]{:S(2)}) collective-permute-start(bf16[4,64,1280]{2,1,0:T(8,128)(2,1)S(1)} %add_convert_fusion.2), channel_id=1, source_target_pairs={{0,8},{2,10},{4,12},{6,14},{8,0},{10,2},{12,4},{14,6},{16,24},{18,... | collective-permute-start | bytes 1966088 | tf_op jit(solution)/shard_map/ppermute | solution.py:759
  212.5 20.1 %collective-permute-start.8 = (bf16[4,64,1280]{2,1,0:T(8,128)(2,1)S(1)}, bf16[4,64,1280]{2,1,0:T(8,128)(2,1)S(1)}, u32[]{:S(2)}, u32[]{:S(2)}) collective-permute-start(bf16[4,64,1280]{2,1,0:T(8,128)(2,1)S(1)} %add_convert_fusion.3), channel_id=1, source_target_pairs={{0,4},{2,6},{4,0},{6,2},{8,12},{10,14},{12,8},{14,10},{16,20},{18,... | collective-permute-start | bytes 1966088 | tf_op jit(solution)/shard_map/ppermute | solution.py:759
  214.5 23.6 %collective-permute-start.16 = (bf16[4,64,1280]{2,1,0:T(8,128)(2,1)S(1)}, bf16[4,64,1280]{2,1,0:T(8,128)(2,1)S(1)}, u32[]{:S(2)}, u32[]{:S(2)}) collective-permute-start(bf16[4,64,1280]{2,1,0:T(8,128)(2,1)S(1)} %add_convert_fusion.1), channel_id=1, source_target_pairs={{0,2},{2,0},{4,6},{6,4},{8,10},{10,8},{12,14},{14,12},{16,18},{18,... | collective-permute-start | bytes 1966088 | tf_op jit(solution)/shard_map/ppermute | solution.py:759
  230.7 22.6 %collective-permute-start.19 = (bf16[8,64,512]{2,1,0:T(8,128)(2,1)}, bf16[8,64,512]{2,1,0:T(8,128)(2,1)S(1)}, u32[]{:S(2)}, u32[]{:S(2)}) collective-permute-start(bf16[8,64,512]{2,1,0:T(8,128)(2,1)} %get-tuple-element.158), channel_id=1, source_target_pairs={{0,4},{2,6},{4,0},{6,2},{8,12},{10,14},{12,8},{14,10},{16,20},{18,... | collective-permute-start | bytes 1572872 | tf_op jit(solution)/shard_map/ppermute | solution.py:759
  232.3 21.0 %collective-permute-start.13 = (bf16[8,64,512]{2,1,0:T(8,128)(2,1)}, bf16[8,64,512]{2,1,0:T(8,128)(2,1)S(1)}, u32[]{:S(2)}, u32[]{:S(2)}) collective-permute-start(bf16[8,64,512]{2,1,0:T(8,128)(2,1)} %get-tuple-element.156), channel_id=1, source_target_pairs={{0,2},{2,0},{4,6},{6,4},{8,10},{10,8},{12,14},{14,12},{16,18},{18,... | collective-permute-start | bytes 1572872 | tf_op jit(solution)/shard_map/ppermute | solution.py:759
  233.7 13.7 %collective-permute-start.14 = (bf16[2,64,1280]{2,1,0:T(8,128)(2,1)S(1)}, bf16[2,64,1280]{2,1,0:T(8,128)(2,1)S(1)}, u32[]{:S(2)}, u32[]{:S(2)}) collective-permute-start(bf16[2,64,1280]{2,1,0:T(8,128)(2,1)S(1)} %add_convert_fusion.7), channel_id=1, source_target_pairs={{0,8},{2,10},{4,12},{6,14},{8,0},{10,2},{12,4},{14,6},{16,24},{18,... | collective-permute-start | bytes 983048 | tf_op jit(solution)/shard_map/ppermute | solution.py:759
  235.5 15.6 %collective-permute-start.15 = (bf16[2,64,1280]{2,1,0:T(8,128)(2,1)S(1)}, bf16[2,64,1280]{2,1,0:T(8,128)(2,1)S(1)}, u32[]{:S(2)}, u32[]{:S(2)}) collective-permute-start(bf16[2,64,1280]{2,1,0:T(8,128)(2,1)S(1)} %add_convert_fusion.6), channel_id=1, source_target_pairs={{0,2},{2,0},{4,6},{6,4},{8,10},{10,8},{12,14},{14,12},{16,18},{18,... | collective-permute-start | bytes 983048 | tf_op jit(solution)/shard_map/ppermute | solution.py:759
  238.1 15.2 %collective-permute-start.20 = (bf16[8,64,512]{2,1,0:T(8,128)(2,1)S(1)}, bf16[8,64,512]{2,1,0:T(8,128)(2,1)S(1)}, u32[]{:S(2)}, u32[]{:S(2)}) collective-permute-start(bf16[8,64,512]{2,1,0:T(8,128)(2,1)S(1)} %copy-done.29), channel_id=1, source_target_pairs={{0,8},{2,10},{4,12},{6,14},{8,0},{10,2},{12,4},{14,6},{16,24},{18,... | collective-permute-start | bytes 1572872 | tf_op jit(solution)/shard_map/ppermute | solution.py:759
  247.3 7.1 %collective-permute-start.18 = (bf16[2,64,1280]{2,1,0:T(8,128)(2,1)S(1)}, bf16[2,64,1280]{2,1,0:T(8,128)(2,1)S(1)}, u32[]{:S(2)}, u32[]{:S(2)}) collective-permute-start(bf16[2,64,1280]{2,1,0:T(8,128)(2,1)S(1)} %get-tuple-element.207), channel_id=1, source_target_pairs={{0,4},{2,6},{4,0},{6,2},{8,12},{10,14},{12,8},{14,10},{16,20},{18,... | collective-permute-start | bytes 983048 | tf_op jit(solution)/shard_map/ppermute | solution.py:759
  254.5 10.5 %collective-permute-start.28 = (bf16[1,64,1280]{2,1,0:T(8,128)(2,1)S(1)}, bf16[1,64,1280]{2,1,0:T(8,128)(2,1)S(1)}, u32[]{:S(2)}, u32[]{:S(2)}) collective-permute-start(bf16[1,64,1280]{2,1,0:T(8,128)(2,1)S(1)} %add_convert_fusion.15), channel_id=1, source_target_pairs={{0,16},{2,18},{4,20},{6,22},{8,24},{10,26},{12,28},{14,30},{16,0},... | collective-permute-start | bytes 491528 | tf_op jit(solution)/shard_map/ppermute | solution.py:759
  258.3 11.4 %collective-permute-start.22 = (bf16[4,64,512]{2,1,0:T(8,128)(2,1)S(1)}, bf16[4,64,512]{2,1,0:T(8,128)(2,1)S(1)}, u32[]{:S(2)}, u32[]{:S(2)}) collective-permute-start(bf16[4,64,512]{2,1,0:T(8,128)(2,1)S(1)} %get-tuple-element.209), channel_id=1, source_target_pairs={{0,8},{2,10},{4,12},{6,14},{8,0},{10,2},{12,4},{14,6},{16,24},{18,... | collective-permute-start | bytes 786440 | tf_op jit(solution)/shard_map/ppermute | solution.py:759
  259.7 9.9 %collective-permute-start.17 = (bf16[4,64,512]{2,1,0:T(8,128)(2,1)S(1)}, bf16[4,64,512]{2,1,0:T(8,128)(2,1)S(1)}, u32[]{:S(2)}, u32[]{:S(2)}) collective-permute-start(bf16[4,64,512]{2,1,0:T(8,128)(2,1)S(1)} %get-tuple-element.211), channel_id=1, source_target_pairs={{0,4},{2,6},{4,0},{6,2},{8,12},{10,14},{12,8},{14,10},{16,20},{18,... | collective-permute-start | bytes 786440 | tf_op jit(solution)/shard_map/ppermute | solution.py:759
  260.3 10.0 %collective-permute-start.23 = (bf16[4,64,512]{2,1,0:T(8,128)(2,1)S(1)}, bf16[4,64,512]{2,1,0:T(8,128)(2,1)S(1)}, u32[]{:S(2)}, u32[]{:S(2)}) collective-permute-start(bf16[4,64,512]{2,1,0:T(8,128)(2,1)S(1)} %get-tuple-element.213), channel_id=1, source_target_pairs={{0,2},{2,0},{4,6},{6,4},{8,10},{10,8},{12,14},{14,12},{16,18},{18,... | collective-permute-start | bytes 786440 | tf_op jit(solution)/shard_map/ppermute | solution.py:759
  260.9 15.8 %collective-permute-start.27 = (bf16[1,64,2560]{2,1,0:T(8,128)(2,1)S(1)}, bf16[1,64,2560]{2,1,0:T(8,128)(2,1)S(1)}, u32[]{:S(2)}, u32[]{:S(2)}) collective-permute-start(bf16[1,64,2560]{2,1,0:T(8,128)(2,1)S(1)} %pad_maximum_fusion), channel_id=1, source_target_pairs={{0,16},{2,18},{4,20},{6,22},{8,24},{10,26},{12,28},{14,30},{16,0},... | collective-permute-start | bytes 983048 | tf_op jit(solution)/shard_map/ppermute | solution.py:759
  269.7 8.1 %collective-permute-start.21 = (bf16[2,64,512]{2,1,0:T(8,128)(2,1)S(1)}, bf16[2,64,512]{2,1,0:T(8,128)(2,1)S(1)}, u32[]{:S(2)}, u32[]{:S(2)}) collective-permute-start(bf16[2,64,512]{2,1,0:T(8,128)(2,1)S(1)} %get-tuple-element.215), channel_id=1, source_target_pairs={{0,8},{2,10},{4,12},{6,14},{8,0},{10,2},{12,4},{14,6},{16,24},{18,... | collective-permute-start | bytes 393224 | tf_op jit(solution)/shard_map/ppermute | solution.py:759
  270.3 7.5 %collective-permute-start.24 = (bf16[2,64,512]{2,1,0:T(8,128)(2,1)S(1)}, bf16[2,64,512]{2,1,0:T(8,128)(2,1)S(1)}, u32[]{:S(2)}, u32[]{:S(2)}) collective-permute-start(bf16[2,64,512]{2,1,0:T(8,128)(2,1)S(1)} %get-tuple-element.217), channel_id=1, source_target_pairs={{0,2},{2,0},{4,6},{6,4},{8,10},{10,8},{12,14},{14,12},{16,18},{18,... | collective-permute-start | bytes 393224 | tf_op jit(solution)/shard_map/ppermute | solution.py:759
  270.8 7.0 %collective-permute-start.25 = (bf16[2,64,512]{2,1,0:T(8,128)(2,1)S(1)}, bf16[2,64,512]{2,1,0:T(8,128)(2,1)S(1)}, u32[]{:S(2)}, u32[]{:S(2)}) collective-permute-start(bf16[2,64,512]{2,1,0:T(8,128)(2,1)S(1)} %get-tuple-element.219), channel_id=1, source_target_pairs={{0,4},{2,6},{4,0},{6,2},{8,12},{10,14},{12,8},{14,10},{16,20},{18,... | collective-permute-start | bytes 393224 | tf_op jit(solution)/shard_map/ppermute | solution.py:759
  277.9 8.7 %collective-permute-start.26 = (bf16[1,64,1536]{2,1,0:T(8,128)(2,1)S(1)}, bf16[1,64,1536]{2,1,0:T(8,128)(2,1)S(1)}, u32[]{:S(2)}, u32[]{:S(2)}) collective-permute-start(bf16[1,64,1536]{2,1,0:T(8,128)(2,1)S(1)} %pad_maximum_fusion.2), channel_id=1, source_target_pairs={{0,16},{2,18},{4,20},{6,22},{8,24},{10,26},{12,28},{14,30},{16,0},... | collective-permute-start | bytes 589832 | tf_op jit(solution)/shard_map/ppermute | solution.py:759
  (36 other events, 409.9 us)

commit v2 on v1

--- a/solution.py
+++ b/solution.py
@@ -360,7 +360,7 @@
                        value_ref, cos_ref, sin_ref,
                        attn_grad_out, projected_out, partial_out,
                        key_total, value_total, query_total, grad_heads, tri_ref):
-    step = pl.num_programs(0) - 1 - pl.program_id(0)
+    pair = pl.num_programs(0) - 1 - pl.program_id(0)
     half = HEAD // 2
 
     @pl.when(pl.program_id(0) == 0)
@@ -373,25 +373,26 @@
     attn_grad = (grad_ref[...].astype(f32) + back).astype(bf16)
     attn_grad_out[...] = attn_grad
     grad_attended = matmul(wout_ref[...], attn_grad).astype(bf16)
-    zeros = jnp.zeros((LANES - HEAD - 8, BLOCK), f32)
+    zeros = jnp.zeros((LANES - HEAD - 8, 2 * BLOCK), f32)
     for s in range(slots):
         for j in range(heads):
             first = (s * heads + j) * HEAD
             mine = grad_attended[first : first + HEAD]
             out = attended_ref[first : first + HEAD, :]
             delta = jnp.sum(mine.astype(f32) * out.astype(f32), axis=0, keepdims=True)
-            lanes = slice(j * BLOCK, (j + 1) * BLOCK)
-            grad_heads[s, :HEAD, lanes] = mine
-            grad_heads[s, HEAD:, lanes] = jnp.concatenate(
-                [part_rows(-delta, 0), zeros], axis=0
-            ).astype(bf16)
-
-    def visit(back):
-        keys = block_at(step - back)
+            rest = jnp.concatenate([part_rows(-delta, 0), zeros], axis=0).astype(bf16)
+            for sub in range(2):
+                lanes = slice(j * BLOCK, (j + 1) * BLOCK)
+                tokens = slice(sub * BLOCK, (sub + 1) * BLOCK)
+                grad_heads[sub, s, :HEAD, lanes] = mine[:, tokens]
+                grad_heads[sub, s, HEAD:, lanes] = rest[:, tokens]
+
+    def visit(sub, back):
+        keys = block_at(2 * pair + sub - back)
         columns = [slice(s * LANES, (s + 1) * LANES) for s in range(slots)]
         features = [slice(s * HEAD, (s + 1) * HEAD) for s in range(slots)]
-        scores = [matmul(key_ref[keys, columns[s]], query_ref[0, s]) for s in range(slots)]
-        grad_weights = [matmul(value_ref[keys, columns[s]], grad_heads[s]) for s in range(slots)]
+        scores = [matmul(key_ref[keys, columns[s]], query_ref[sub, s]) for s in range(slots)]
+        grad_weights = [matmul(value_ref[keys, columns[s]], grad_heads[sub, s]) for s in range(slots)]
         weights, grad_scores = [], []
         for s in range(slots):
             score = scores[s] + tri_ref[...] if back == 0 else scores[s]
@@ -399,24 +400,27 @@
             weights.append(weight.astype(bf16))
             grad_scores.append((weight * grad_weights[s]).astype(bf16))
         for s in range(slots):
-            value_total[features[s], keys] += matmul(grad_heads[s, :HEAD, :], weights[s], NT)
-            key_total[features[s], keys] += matmul(query_ref[0, s, :HEAD, :], grad_scores[s], NT)
+            value_total[features[s], keys] += matmul(grad_heads[sub, s, :HEAD, :], weights[s], NT)
+            key_total[features[s], keys] += matmul(query_ref[sub, s, :HEAD, :], grad_scores[s], NT)
             update = matmul(turned_key_ref[features[s], keys], grad_scores[s])
             if back == 0:
-                query_total[s] = update
+                query_total[sub, s] = update
             else:
-                query_total[s] += update
-
-    visit(0)
-    for back in (1, 2):
-        pl.when(reaches(segments, step, back))(functools.partial(visit, back))
+                query_total[sub, s] += update
+
+    for sub in (1, 0):
+        visit(sub, 0)
+        for back in (1, 2):
+            pl.when(reaches(segments, 2 * pair + sub, back))(functools.partial(visit, sub, back))
 
     cosine, sine = cos_ref[...], sin_ref[...]
-    here = block_at(step)
+    here = pl.ds(pl.multiple_of(pair * 2 * BLOCK, 2 * BLOCK), 2 * BLOCK)
     for s in range(slots):
         for j in range(heads + 2):
             if j < heads:
-                piece = query_total[s, :, j * BLOCK : (j + 1) * BLOCK] * (1.0 / math.sqrt(HEAD))
+                lanes = slice(j * BLOCK, (j + 1) * BLOCK)
+                piece = jnp.concatenate([query_total[sub, s, :, lanes] for sub in range(2)], axis=1)
+                piece = piece * (1.0 / math.sqrt(HEAD))
             elif j == heads:
                 piece = key_total[s * HEAD : (s + 1) * HEAD, here] * LN2
             else:
@@ -432,12 +436,12 @@
 def call_attention_backward(segments, grad, own, other, normed, inverse, gain, wout, wqkv, attended, query,
                             key, turned_key, value, cosine, sine):
     features, length = grad.shape
-    count = length // BLOCK
+    count = length // (2 * BLOCK)
     slots, wide_heads = query.shape[1], query.shape[3]
     heads = wide_heads // BLOCK
 
     def spec(rows):
-        return pl.BlockSpec((rows, BLOCK), lambda i, *_: (0, count - 1 - i))
+        return pl.BlockSpec((rows, 2 * BLOCK), lambda i, *_: (0, count - 1 - i))
 
     return pl.pallas_call(
         functools.partial(attention_backward, slots, heads),
@@ -447,15 +451,15 @@
             in_specs=[spec(features)] * 4 + [spec(1)]
             + [full_spec(a.shape) for a in (gain, wout, wqkv)]
             + [spec(attended.shape[0])]
-            + [pl.BlockSpec((1, slots, LANES, wide_heads), lambda i, *_: (count - 1 - i, 0, 0, 0))]
+            + [pl.BlockSpec((2, slots, LANES, wide_heads), lambda i, *_: (count - 1 - i, 0, 0, 0))]
             + [full_spec(a.shape) for a in (key, turned_key, value)]
             + [spec(HEAD // 2)] * 2,
             out_specs=[spec(features), spec(wqkv.shape[0]), spec(features)],
             scratch_shapes=[
                 pltpu.VMEM((slots * HEAD, length), f32),
                 pltpu.VMEM((slots * HEAD, length), f32),
-                pltpu.VMEM((slots, HEAD, wide_heads), f32),
-                pltpu.VMEM((slots, LANES, wide_heads), bf16),
+                pltpu.VMEM((2, slots, HEAD, wide_heads), f32),
+                pltpu.VMEM((2, slots, LANES, wide_heads), bf16),
                 pltpu.VMEM((BLOCK, wide_heads), f32),
             ],
         ),
@@ -463,7 +467,7 @@
             shape_of((features, length), bf16), shape_of((wqkv.shape[0], length), bf16),
             anywhere((features, length), bf16),
         ],
-        compiler_params=pltpu.CompilerParams(vmem_limit_bytes=30 * MIB),
+        compiler_params=pltpu.CompilerParams(vmem_limit_bytes=33 * MIB),
         cost_estimate=cost(2 * length * features * (wqkv.shape[0] + wout.shape[0]) + slots * 8e9, grad),
         name="attention_backward",
     )(segments, *in_hbm(grad), own, other, *in_hbm(normed), inverse, gain, wout, wqkv,
@@ -845,7 +849,10 @@
     parts = (tokens_in[0].T,)
     saved = []
     for _ in range(REPEAT):
-        outs = list(call_attention_forward(segments, parts, gain_one, wqkv, wout, cosine, sine, slots, heads))
+        own_weights = (wqkv, wout) if len(parts) == 3 else in_hbm(wqkv, wout)
+        outs = list(
+            call_attention_forward(segments, parts, gain_one, *own_weights, cosine, sine, slots, heads)
+        )
         hidden = outs.pop(0) if len(parts) == 3 else parts[0]
         normed, inverse, query, key, turned_key, value, attended, partial = outs
         middle, normed_two, inverse_two, gate, lift, inner, partial_two = call_ffn_forward(

time: 295 us -> 293 us (level)
    pallas_call x2, Pallas kernels: 32.2 us -> 43.5 us  [call_attention_forward(): pl.pallas_call(functools.partial(attention_forward, joined, slots, heads)...]
    pallas_call x2, Pallas kernels: 37.9 us -> 27.3 us  [call_ffn_backward(): pl.pallas_call(functools.partial(ffn_backward, bool(joint)), grid=(length...]
    unnamed x64 -> x60, local copies, waits for them, and re-layouts: 6.29 us -> 3.49 us
  transfers between devices with their start and end apart: 30 -> 30, of which waited for: 14 -> 13; matrix products, arithmetic and copies ran while one was open for 8% -> 8% of each run, Pallas kernels for 32% -> 28%
where the time goes in v2:
time: 293 us; the launch traced here: 290 us
  Pallas kernels  194 us (66%)
  waiting for transfers between devices  42.2 us (14%)
  starting transfers between devices  26.9 us (9%)
  other arithmetic  19.2 us (7%)
  local copies, waits for them, and re-layouts  4.89 us (2%)
    pallas_call x2, Pallas kernels, call_attention_backward(): pl.pallas_call(functools.partial(attention_backward, slots, heads), grid_...  47.8 us
    pallas_call x2, Pallas kernels, call_attention_forward(): pl.pallas_call(functools.partial(attention_forward, joined, slots, heads)...  43.5 us
    pallas_call x2, Pallas kernels, call_weight_grad(): pl.pallas_call(functools.partial(kernel, orders, rows), grid_spec=pltpu.P...  38.8 us
    pallas_call x2, Pallas kernels, call_ffn_backward(): pl.pallas_call(functools.partial(ffn_backward, bool(joint)), grid=(length...  27.3 us
    pallas_call x2, Pallas kernels, call_ffn_forward(): pl.pallas_call(ffn_forward, grid=(length // FFN_BLOCK,), in_specs=[spec(f...  26.3 us
    ppermute x21, waiting for transfers between devices, transfer(): lax.ppermute(sent, 'dp', [(i, i ^ 1 << bit) for i in range(size)])  25.9 us
    ppermute x21, starting transfers between devices, transfer(): lax.ppermute(sent, 'dp', [(i, i ^ 1 << bit) for i in range(size)])  25 us
    ppermute x9, waiting for transfers between devices, exchange(): return lax.ppermute(own, 'mp', [(0, 1), (1, 0)])  16.3 us
  transfers between devices with their start and end apart: 30, of which 13 were waited for; matrix products, arithmetic and copies ran while one was open for 8% of the time, Pallas kernels for 28%

profile of v2, /device:TPU:0, one launch (start us, length us, event | category | flops | bytes accessed | tf_op | source)
XLA Modules:
  0.0 289.9 jit_solution(16472359535382094311)
XLA Ops:
  0.7 4.5 %gather_groups.1 = (bf16[960,960]{1,0:T(8,128)(2,1)}, bf16[576,960]{1,0:T(8,128)(2,1)}) custom-call(s32[5]{0:T(128)} %owner.1, s32[1]{0:T(128)} %bitcast.4.device, bf16[5,192,960]{2,1,0:T(8,128)(2,1)} %bitcast.61, bf16[5,64,960]{2,1,0:T(8,128)(2,1)} %bitcast.62, bf16[5,64,960]{2,1,0:T(8,128)(2,1)} %bitcast.63, bf16[5,192,960]{2,1,0:T(8,128)(2,1)} %refs_3_.2), custom_call_target="tpu_custom_call" | custom-call | tf_op jit(solution)/shard_map/gather_groups/pallas_call | solution.py:704
  5.4 16.3 %attention_forward.2 = (bf16[960,1024]{1,0:T(8,128)(2,1)}, f32[1,1024]{1,0:T(1,128)}, bf16[4,3,128,768]{3,2,1,0:T(8,128)(2,1)}, bf16[1024,384]{1,0:T(8,128)(2,1)...) custom-call(s32[1024]{0:T(1024)S(1)} %bitcast.53, ...), custom_call_target="tpu_custom_call" | custom-call | flops 15019898880 | bytes 1966080 | tf_op jit(solution)/shard_map/attention_forward/pallas_call | solution.py:251
  22.0 3.8 %collective-permute-done.other_ref = bf16[960,1024]{1,0:T(8,128)(2,1)S(1)} collective-permute-done((bf16[960,1024]{1,0:T(8,128)(2,1)S(1)}, bf16[960,1024]{1,0:T(8,128)(2,1)S(1)}, u32[]{:S(2)}, u32[]{:S(2)}) %collective-permute-start) | collective-permute-done | bytes 1966112 | tf_op jit(solution)/shard_map/ppermute | solution.py:726
  26.0 13.2 %ffn_forward.2 = (f32[960,1024]{1,0:T(8,128)}, bf16[960,1024]{1,0:T(8,128)(2,1)}, f32[1,1024]{1,0:T(1,128)}, bf16[2,1280,512]{2,1,0:T(8,128)(2,1)}, bf16[2,1280,...) custom-call(bf16[960,1024]{1,0:T(8,128)(2,1)} %bitcast.69, ...), custom_call_target="tpu_custom_call" | custom-call | flops 7549747200 | bytes 1966080 | tf_op jit(solution)/shard_map/ffn_forward/pallas_call | solution.py:292
  39.3 3.8 %collective-permute-done.1.refs_2_ = bf16[960,1024]{1,0:T(8,128)(2,1)S(1)} collective-permute-done((bf16[960,1024]{1,0:T(8,128)(2,1)S(1)}, bf16[960,1024]{1,0:T(8,128)(2,1)S(1)}, u32[]{:S(2)}, u32[]{:S(2)}) %collective-permute-start.1) | collective-permute-done | bytes 1966112 | tf_op jit(solution)/shard_map/ppermute | solution.py:726
  43.2 27.2 %attention_forward.3 = (f32[960,1024]{1,0:T(8,128)}, bf16[960,1024]{1,0:T(8,128)(2,1)}, f32[1,1024]{1,0:T(1,128)}, bf16[4,3,128,768]{3,2,1,0:T(8,128)(2,1)}, bf1...) custom-call(s32[1024]{0:T(1024)S(1)} %bitcast.54, ...), custom_call_target="tpu_custom_call" | custom-call | flops 15019898880 | bytes 7864320 | tf_op jit(solution)/shard_map/attention_forward/pallas_call | solution.py:251
  70.6 3.8 %collective-permute-done.2.other_ref = bf16[960,1024]{1,0:T(8,128)(2,1)S(1)} collective-permute-done((bf16[960,1024]{1,0:T(8,128)(2,1)S(1)}, bf16[960,1024]{1,0:T(8,128)(2,1)S(1)}, u32[]{:S(2)}, u32[]{:S(2)}) %collective-permute-start.2) | collective-permute-done | bytes 1966112 | tf_op jit(solution)/shard_map/ppermute | solution.py:726
  74.4 13.1 %ffn_forward.3 = (f32[960,1024]{1,0:T(8,128)}, bf16[960,1024]{1,0:T(8,128)(2,1)}, f32[1,1024]{1,0:T(1,128)}, bf16[2,1280,512]{2,1,0:T(8,128)(2,1)}, bf16[2,1280,...) custom-call(f32[960,1024]{1,0:T(8,128)} %get-tuple-element.101.hidden_ref, ...), custom_call_target="tpu_custom_call" | custom-call | flops 7549747200 | bytes 3932160 | tf_op jit(solution)/shard_map/ffn_forward/pallas_call | solution.py:292
  87.7 11.8 %ffn_backward.2 = (bf16[2,1280,512]{2,1,0:T(8,128)(2,1)}, bf16[2,1280,512]{2,1,0:T(8,128)(2,1)}, bf16[960,1024]{1,0:T(8,128)(2,1)S(1)}) custom-call(bf16[960,1024]{1,0:T(8,128)(2,1)} %bitcast.70, bf16[2,1280,512]{2,1,0:T(8,128)(2,1)} %get-tuple-element.105.refs_0_, bf16[2,1280,512]{2,1,0:T(8,128)(2,1)} %get-tuple-element.106.refs_1_, ...), custom_call_target="tpu_custom_call" | custom-call | flops 7549747200 | bytes 1966080 | tf_op jit(solution)/shard_map/ffn_backward/pallas_call | solution.py:345
  99.8 2.4 add_convert_fusion
  103.4 23.4 %attention_backward.2 = (bf16[960,1024]{1,0:T(8,128)(2,1)}, bf16[960,1024]{1,0:T(8,128)(2,1)}, bf16[960,1024]{1,0:T(8,128)(2,1)S(1)}) custom-call(s32[1024]{0:T(1024)S(1)} %bitcast.55, bf16[960,1024]{1,0:T(8,128)(2,1)} %bitcast.71, bf16[960,1024]{1,0:T(8,128)(2,1)S(1)} %get-tuple-element.107.own_ref, bf16[960,1024]{1,0:T(8,128)(2,1)S(1)} %collective-permute-done.4.other_ref, ...), custom_call_target="tpu_custom_call" | custom-call | flops 27019898880 | bytes 1966080 | tf_op jit(solution)/shard_map/attention_backward/pallas_call | solution.py:446
  127.2 3.6 %collective-permute-done.5.refs_3_ = bf16[960,1024]{1,0:T(8,128)(2,1)S(1)} collective-permute-done((bf16[960,1024]{1,0:T(8,128)(2,1)S(1)}, bf16[960,1024]{1,0:T(8,128)(2,1)S(1)}, u32[]{:S(2)}, u32[]{:S(2)}) %collective-permute-start.5) | collective-permute-done | bytes 1966112 | tf_op jit(solution)/shard_map/ppermute | solution.py:726
  130.8 15.5 %ffn_backward.3 = (bf16[960,1024]{1,0:T(8,128)(2,1)}, bf16[2,1280,512]{2,1,0:T(8,128)(2,1)}, bf16[2,1280,512]{2,1,0:T(8,128)(2,1)}, bf16[960,1024]{1,0:T(8,128)(2,1)}) custom-call(bf16[960,1024]{1,0:T(8,128)(2,1)} %get-tuple-element.119.grad_ref.refs_4_, bf16[960,1024]{1,0:T(8,128)(2,1)} %get-tuple-element.120.refs_0_, f32[1,1024]{1,0:T(1,128)S(1)} %copy-done.16, ...), custom_call_target="tpu_custom_call" | custom-call | flops 7549747200 | bytes 1966080 | tf_op jit(solution)/shard_map/ffn_backward/pallas_call | solution.py:345
  146.8 24.3 %ffn_weight_grad.1 = (bf16[8,64,1280]{2,1,0:T(8,128)(2,1)}, bf16[8,64,1280]{2,1,0:T(8,128)(2,1)}, bf16[8,64,1280]{2,1,0:T(8,128)(2,1)}, bf16[8,64,1280]{2,1,0:T(...) custom-call(s32[3]{0:T(128)S(1)} %pad_add_fusion.bits, ...), custom_call_target="tpu_custom_call" | custom-call | flops 15099494400 | bytes 23592960 | tf_op jit(solution)/shard_map/ffn_weight_grad/pallas_call | solution.py:572
  171.1 3.1 %collective-permute-start.10 = (bf16[8,64,1280]{2,1,0:T(8,128)(2,1)}, bf16[8,64,1280]{2,1,0:T(8,128)(2,1)}, u32[]{:S(2)}, u32[]{:S(2)}) collective-permute-start(bf16[8,64,1280]{2,1,0:T(8,128)(2,1)} %get-tuple-element.139), channel_id=1, source_target_pairs={{0,8},{2,10},{4,12},{6,14},{8,0},{10,2},{12,4},{14,6},{16,24},{18,... | collective-permute-start | bytes 3932168 | tf_op jit(solution)/shard_map/ppermute | solution.py:763
  175.7 24.4 %attention_backward.3 = (bf16[960,1024]{1,0:T(8,128)(2,1)}, bf16[960,1024]{1,0:T(8,128)(2,1)}, bf16[960,1024]{1,0:T(8,128)(2,1)}) custom-call(s32[1024]{0:T(1024)S(1)} %bitcast.56, bf16[960,1024]{1,0:T(8,128)(2,1)} %get-tuple-element.125.refs_7_.grad_ref, bf16[960,1024]{1,0:T(8,128)(2,1)} %get-tuple-element.140.own_ref, ...), custom_call_target="tpu_custom_call" | custom-call | flops 27019898880 | bytes 1966080 | tf_op jit(solution)/shard_map/attention_backward/pallas_call | solution.py:446
  212.8 14.5 %attention_weight_grad.1 = (bf16[8,64,512]{2,1,0:T(8,128)(2,1)}, bf16[8,64,512]{2,1,0:T(8,128)(2,1)}, bf16[8,64,512]{2,1,0:T(8,128)(2,1)}, bf16[8,64,512]{2,1,0:...) custom-call(s32[3]{0:T(128)S(1)} %pad_add_fusion.bits, ...), custom_call_target="tpu_custom_call" | custom-call | flops 6039797760 | bytes 14155776 | tf_op jit(solution)/shard_map/attention_weight_grad/pallas_call | solution.py:572
  236.5 6.1 %block_grad.1 = f32[960,1024]{1,0:T(8,128)} custom-call(bf16[960,1024]{1,0:T(8,128)(2,1)} %get-tuple-element.164.refs_5_.grad_ref, bf16[960,1024]{1,0:T(8,128)(2,1)} %get-tuple-element.150.refs_1_.normed_ref, f32[1,1024]{1,0:T(1,128)S(1)} %copy-done.3, bf16[960,1024]{1,0:T(8,128)(2,1)} %get-tuple-element.161.own_ref, ...), custom_call_target="tpu_custom_call" | custom-call | bytes 7864320 | tf_op jit(solution)/shard_map/block_grad/pallas_call | solution.py:653
  244.6 3.0 %collective-permute-done.15 = bf16[2,64,1280]{2,1,0:T(8,128)(2,1)S(1)} collective-permute-done((bf16[2,64,1280]{2,1,0:T(8,128)(2,1)S(1)}, bf16[2,64,1280]{2,1,0:T(8,128)(2,1)S(1)}, u32[]{:S(2)}, u32[]{:S(2)}) %collective-permute-start.15) | collective-permute-done | bytes 327712 | tf_op jit(solution)/shard_map/ppermute | solution.py:763
  251.2 2.7 collective-permute-start.28
  257.9 5.6 %collective-permute-done.28 = bf16[1,64,1280]{2,1,0:T(8,128)(2,1)S(1)} collective-permute-done((bf16[1,64,1280]{2,1,0:T(8,128)(2,1)S(1)}, bf16[1,64,1280]{2,1,0:T(8,128)(2,1)S(1)}, u32[]{:S(2)}, u32[]{:S(2)}) %collective-permute-start.28) | collective-permute-done | bytes 163872 | tf_op jit(solution)/shard_map/ppermute | solution.py:763
  264.3 2.5 collective-permute-start.21
  268.2 7.2 %collective-permute-done.27 = bf16[1,64,2560]{2,1,0:T(8,128)(2,1)S(1)} collective-permute-done((bf16[1,64,2560]{2,1,0:T(8,128)(2,1)S(1)}, bf16[1,64,2560]{2,1,0:T(8,128)(2,1)S(1)}, u32[]{:S(2)}, u32[]{:S(2)}) %collective-permute-start.27) | collective-permute-done | bytes 327712 | tf_op jit(solution)/shard_map/ppermute | solution.py:763
  279.7 4.9 %collective-permute-done.26 = bf16[1,64,1536]{2,1,0:T(8,128)(2,1)S(1)} collective-permute-done((bf16[1,64,1536]{2,1,0:T(8,128)(2,1)S(1)}, bf16[1,64,1536]{2,1,0:T(8,128)(2,1)S(1)}, u32[]{:S(2)}, u32[]{:S(2)}) %collective-permute-start.26) | collective-permute-done | bytes 196640 | tf_op jit(solution)/shard_map/ppermute | solution.py:763
  (151 shorter events, 47.6 us)
Async XLA Ops:
  87.5 12.3 %collective-permute-start.3 = (bf16[960,1024]{1,0:T(8,128)(2,1)S(1)}, bf16[960,1024]{1,0:T(8,128)(2,1)S(1)}, u32[]{:S(2)}, u32[]{:S(2)}) collective-permute-start(bf16[960,1024]{1,0:T(8,128)(2,1)S(1)} %get-tuple-element.109), channel_id=1, source_target_pairs={{0,1},{1,0},{2,3},{3,2},{4,5},{5,4},{6,7},{7,6},{8,9},{9,8},{10,11... | collective-permute-start | bytes 5898248 | tf_op jit(solution)/shard_map/ppermute | solution.py:726
  146.3 29.3 %collective-permute-start.6 = (bf16[960,1024]{1,0:T(8,128)(2,1)}, bf16[960,1024]{1,0:T(8,128)(2,1)}, u32[]{:S(2)}, u32[]{:S(2)}) collective-permute-start(bf16[960,1024]{1,0:T(8,128)(2,1)} %get-tuple-element.140.own_ref), channel_id=1, source_target_pairs={{0,1},{1,0},{2,3},{3,2},{4,5},{5,4},{6,7},{7,6},{8,9},{9,8},{10,11... | collective-permute-start | bytes 5898248 | tf_op jit(solution)/shard_map/ppermute | solution.py:726
  171.1 32.5 %collective-permute-start.10 = (bf16[8,64,1280]{2,1,0:T(8,128)(2,1)}, bf16[8,64,1280]{2,1,0:T(8,128)(2,1)}, u32[]{:S(2)}, u32[]{:S(2)}) collective-permute-start(bf16[8,64,1280]{2,1,0:T(8,128)(2,1)} %get-tuple-element.139), channel_id=1, source_target_pairs={{0,8},{2,10},{4,12},{6,14},{8,0},{10,2},{12,4},{14,6},{16,24},{18,... | collective-permute-start | bytes 3932168 | tf_op jit(solution)/shard_map/ppermute | solution.py:763
  174.2 30.9 %collective-permute-start.9 = (bf16[8,64,1280]{2,1,0:T(8,128)(2,1)}, bf16[8,64,1280]{2,1,0:T(8,128)(2,1)}, u32[]{:S(2)}, u32[]{:S(2)}) collective-permute-start(bf16[8,64,1280]{2,1,0:T(8,128)(2,1)} %get-tuple-element.137), channel_id=1, source_target_pairs={{0,4},{2,6},{4,0},{6,2},{8,12},{10,14},{12,8},{14,10},{16,20},{18,... | collective-permute-start | bytes 3932168 | tf_op jit(solution)/shard_map/ppermute | solution.py:763
  175.7 30.6 %collective-permute-start.7 = (bf16[8,64,1280]{2,1,0:T(8,128)(2,1)}, bf16[8,64,1280]{2,1,0:T(8,128)(2,1)}, u32[]{:S(2)}, u32[]{:S(2)}) collective-permute-start(bf16[8,64,1280]{2,1,0:T(8,128)(2,1)} %get-tuple-element.135), channel_id=1, source_target_pairs={{0,2},{2,0},{4,6},{6,4},{8,10},{10,8},{12,14},{14,12},{16,18},{18,... | collective-permute-start | bytes 3932168 | tf_op jit(solution)/shard_map/ppermute | solution.py:763
  200.1 29.4 %collective-permute-start.11 = (bf16[960,1024]{1,0:T(8,128)(2,1)}, bf16[960,1024]{1,0:T(8,128)(2,1)}, u32[]{:S(2)}, u32[]{:S(2)}) collective-permute-start(bf16[960,1024]{1,0:T(8,128)(2,1)} %get-tuple-element.161.own_ref), channel_id=1, source_target_pairs={{0,1},{1,0},{2,3},{3,2},{4,5},{5,4},{6,7},{7,6},{8,9},{9,8},{10,11... | collective-permute-start | bytes 5898248 | tf_op jit(solution)/shard_map/ppermute | solution.py:726
  207.7 21.3 %collective-permute-start.12 = (bf16[4,64,1280]{2,1,0:T(8,128)(2,1)S(1)}, bf16[4,64,1280]{2,1,0:T(8,128)(2,1)S(1)}, u32[]{:S(2)}, u32[]{:S(2)}) collective-permute-start(bf16[4,64,1280]{2,1,0:T(8,128)(2,1)S(1)} %add_convert_fusion.2), channel_id=1, source_target_pairs={{0,8},{2,10},{4,12},{6,14},{8,0},{10,2},{12,4},{14,6},{16,24},{18,... | collective-permute-start | bytes 1966088 | tf_op jit(solution)/shard_map/ppermute | solution.py:763
  209.5 20.1 %collective-permute-start.8 = (bf16[4,64,1280]{2,1,0:T(8,128)(2,1)S(1)}, bf16[4,64,1280]{2,1,0:T(8,128)(2,1)S(1)}, u32[]{:S(2)}, u32[]{:S(2)}) collective-permute-start(bf16[4,64,1280]{2,1,0:T(8,128)(2,1)S(1)} %add_convert_fusion.3), channel_id=1, source_target_pairs={{0,4},{2,6},{4,0},{6,2},{8,12},{10,14},{12,8},{14,10},{16,20},{18,... | collective-permute-start | bytes 1966088 | tf_op jit(solution)/shard_map/ppermute | solution.py:763
  211.3 23.5 %collective-permute-start.16 = (bf16[4,64,1280]{2,1,0:T(8,128)(2,1)S(1)}, bf16[4,64,1280]{2,1,0:T(8,128)(2,1)S(1)}, u32[]{:S(2)}, u32[]{:S(2)}) collective-permute-start(bf16[4,64,1280]{2,1,0:T(8,128)(2,1)S(1)} %add_convert_fusion.1), channel_id=1, source_target_pairs={{0,2},{2,0},{4,6},{6,4},{8,10},{10,8},{12,14},{14,12},{16,18},{18,... | collective-permute-start | bytes 1966088 | tf_op jit(solution)/shard_map/ppermute | solution.py:763
  227.4 22.3 %collective-permute-start.19 = (bf16[8,64,512]{2,1,0:T(8,128)(2,1)}, bf16[8,64,512]{2,1,0:T(8,128)(2,1)S(1)}, u32[]{:S(2)}, u32[]{:S(2)}) collective-permute-start(bf16[8,64,512]{2,1,0:T(8,128)(2,1)} %get-tuple-element.158), channel_id=1, source_target_pairs={{0,4},{2,6},{4,0},{6,2},{8,12},{10,14},{12,8},{14,10},{16,20},{18,... | collective-permute-start | bytes 1572872 | tf_op jit(solution)/shard_map/ppermute | solution.py:763
  229.0 20.8 %collective-permute-start.13 = (bf16[8,64,512]{2,1,0:T(8,128)(2,1)}, bf16[8,64,512]{2,1,0:T(8,128)(2,1)S(1)}, u32[]{:S(2)}, u32[]{:S(2)}) collective-permute-start(bf16[8,64,512]{2,1,0:T(8,128)(2,1)} %get-tuple-element.156), channel_id=1, source_target_pairs={{0,2},{2,0},{4,6},{6,4},{8,10},{10,8},{12,14},{14,12},{16,18},{18,... | collective-permute-start | bytes 1572872 | tf_op jit(solution)/shard_map/ppermute | solution.py:763
  230.6 13.4 %collective-permute-start.14 = (bf16[2,64,1280]{2,1,0:T(8,128)(2,1)S(1)}, bf16[2,64,1280]{2,1,0:T(8,128)(2,1)S(1)}, u32[]{:S(2)}, u32[]{:S(2)}) collective-permute-start(bf16[2,64,1280]{2,1,0:T(8,128)(2,1)S(1)} %add_convert_fusion.7), channel_id=1, source_target_pairs={{0,8},{2,10},{4,12},{6,14},{8,0},{10,2},{12,4},{14,6},{16,24},{18,... | collective-permute-start | bytes 983048 | tf_op jit(solution)/shard_map/ppermute | solution.py:763
  233.4 14.1 %collective-permute-start.15 = (bf16[2,64,1280]{2,1,0:T(8,128)(2,1)S(1)}, bf16[2,64,1280]{2,1,0:T(8,128)(2,1)S(1)}, u32[]{:S(2)}, u32[]{:S(2)}) collective-permute-start(bf16[2,64,1280]{2,1,0:T(8,128)(2,1)S(1)} %add_convert_fusion.6), channel_id=1, source_target_pairs={{0,2},{2,0},{4,6},{6,4},{8,10},{10,8},{12,14},{14,12},{16,18},{18,... | collective-permute-start | bytes 983048 | tf_op jit(solution)/shard_map/ppermute | solution.py:763
  234.8 15.0 %collective-permute-start.20 = (bf16[8,64,512]{2,1,0:T(8,128)(2,1)S(1)}, bf16[8,64,512]{2,1,0:T(8,128)(2,1)S(1)}, u32[]{:S(2)}, u32[]{:S(2)}) collective-permute-start(bf16[8,64,512]{2,1,0:T(8,128)(2,1)S(1)} %copy-done.27), channel_id=1, source_target_pairs={{0,8},{2,10},{4,12},{6,14},{8,0},{10,2},{12,4},{14,6},{16,24},{18,... | collective-permute-start | bytes 1572872 | tf_op jit(solution)/shard_map/ppermute | solution.py:763
  244.0 7.1 %collective-permute-start.18 = (bf16[2,64,1280]{2,1,0:T(8,128)(2,1)S(1)}, bf16[2,64,1280]{2,1,0:T(8,128)(2,1)S(1)}, u32[]{:S(2)}, u32[]{:S(2)}) collective-permute-start(bf16[2,64,1280]{2,1,0:T(8,128)(2,1)S(1)} %get-tuple-element.207), channel_id=1, source_target_pairs={{0,4},{2,6},{4,0},{6,2},{8,12},{10,14},{12,8},{14,10},{16,20},{18,... | collective-permute-start | bytes 983048 | tf_op jit(solution)/shard_map/ppermute | solution.py:763
  251.2 12.2 %collective-permute-start.28 = (bf16[1,64,1280]{2,1,0:T(8,128)(2,1)S(1)}, bf16[1,64,1280]{2,1,0:T(8,128)(2,1)S(1)}, u32[]{:S(2)}, u32[]{:S(2)}) collective-permute-start(bf16[1,64,1280]{2,1,0:T(8,128)(2,1)S(1)} %add_convert_fusion.15), channel_id=1, source_target_pairs={{0,16},{2,18},{4,20},{6,22},{8,24},{10,26},{12,28},{14,30},{16,0},... | collective-permute-start | bytes 491528 | tf_op jit(solution)/shard_map/ppermute | solution.py:763
  254.8 9.4 %collective-permute-start.22 = (bf16[4,64,512]{2,1,0:T(8,128)(2,1)S(1)}, bf16[4,64,512]{2,1,0:T(8,128)(2,1)S(1)}, u32[]{:S(2)}, u32[]{:S(2)}) collective-permute-start(bf16[4,64,512]{2,1,0:T(8,128)(2,1)S(1)} %get-tuple-element.209), channel_id=1, source_target_pairs={{0,8},{2,10},{4,12},{6,14},{8,0},{10,2},{12,4},{14,6},{16,24},{18,... | collective-permute-start | bytes 786440 | tf_op jit(solution)/shard_map/ppermute | solution.py:763
  256.5 7.8 %collective-permute-start.17 = (bf16[4,64,512]{2,1,0:T(8,128)(2,1)S(1)}, bf16[4,64,512]{2,1,0:T(8,128)(2,1)S(1)}, u32[]{:S(2)}, u32[]{:S(2)}) collective-permute-start(bf16[4,64,512]{2,1,0:T(8,128)(2,1)S(1)} %get-tuple-element.211), channel_id=1, source_target_pairs={{0,4},{2,6},{4,0},{6,2},{8,12},{10,14},{12,8},{14,10},{16,20},{18,... | collective-permute-start | bytes 786440 | tf_op jit(solution)/shard_map/ppermute | solution.py:763
  257.0 9.9 %collective-permute-start.23 = (bf16[4,64,512]{2,1,0:T(8,128)(2,1)S(1)}, bf16[4,64,512]{2,1,0:T(8,128)(2,1)S(1)}, u32[]{:S(2)}, u32[]{:S(2)}) collective-permute-start(bf16[4,64,512]{2,1,0:T(8,128)(2,1)S(1)} %get-tuple-element.213), channel_id=1, source_target_pairs={{0,2},{2,0},{4,6},{6,4},{8,10},{10,8},{12,14},{14,12},{16,18},{18,... | collective-permute-start | bytes 786440 | tf_op jit(solution)/shard_map/ppermute | solution.py:763
  257.3 18.1 %collective-permute-start.27 = (bf16[1,64,2560]{2,1,0:T(8,128)(2,1)S(1)}, bf16[1,64,2560]{2,1,0:T(8,128)(2,1)S(1)}, u32[]{:S(2)}, u32[]{:S(2)}) collective-permute-start(bf16[1,64,2560]{2,1,0:T(8,128)(2,1)S(1)} %pad_maximum_fusion), channel_id=1, source_target_pairs={{0,16},{2,18},{4,20},{6,22},{8,24},{10,26},{12,28},{14,30},{16,0},... | collective-permute-start | bytes 983048 | tf_op jit(solution)/shard_map/ppermute | solution.py:763
  264.3 11.2 %collective-permute-start.21 = (bf16[2,64,512]{2,1,0:T(8,128)(2,1)S(1)}, bf16[2,64,512]{2,1,0:T(8,128)(2,1)S(1)}, u32[]{:S(2)}, u32[]{:S(2)}) collective-permute-start(bf16[2,64,512]{2,1,0:T(8,128)(2,1)S(1)} %get-tuple-element.215), channel_id=1, source_target_pairs={{0,8},{2,10},{4,12},{6,14},{8,0},{10,2},{12,4},{14,6},{16,24},{18,... | collective-permute-start | bytes 393224 | tf_op jit(solution)/shard_map/ppermute | solution.py:763
  266.9 8.6 %collective-permute-start.24 = (bf16[2,64,512]{2,1,0:T(8,128)(2,1)S(1)}, bf16[2,64,512]{2,1,0:T(8,128)(2,1)S(1)}, u32[]{:S(2)}, u32[]{:S(2)}) collective-permute-start(bf16[2,64,512]{2,1,0:T(8,128)(2,1)S(1)} %get-tuple-element.217), channel_id=1, source_target_pairs={{0,2},{2,0},{4,6},{6,4},{8,10},{10,8},{12,14},{14,12},{16,18},{18,... | collective-permute-start | bytes 393224 | tf_op jit(solution)/shard_map/ppermute | solution.py:763
  267.5 8.0 %collective-permute-start.25 = (bf16[2,64,512]{2,1,0:T(8,128)(2,1)S(1)}, bf16[2,64,512]{2,1,0:T(8,128)(2,1)S(1)}, u32[]{:S(2)}, u32[]{:S(2)}) collective-permute-start(bf16[2,64,512]{2,1,0:T(8,128)(2,1)S(1)} %get-tuple-element.219), channel_id=1, source_target_pairs={{0,4},{2,6},{4,0},{6,2},{8,12},{10,14},{12,8},{14,10},{16,20},{18,... | collective-permute-start | bytes 393224 | tf_op jit(solution)/shard_map/ppermute | solution.py:763
  275.6 9.1 %collective-permute-start.26 = (bf16[1,64,1536]{2,1,0:T(8,128)(2,1)S(1)}, bf16[1,64,1536]{2,1,0:T(8,128)(2,1)S(1)}, u32[]{:S(2)}, u32[]{:S(2)}) collective-permute-start(bf16[1,64,1536]{2,1,0:T(8,128)(2,1)S(1)} %pad_maximum_fusion.2), channel_id=1, source_target_pairs={{0,16},{2,18},{4,20},{6,22},{8,24},{10,26},{12,28},{14,30},{16,0},... | collective-permute-start | bytes 589832 | tf_op jit(solution)/shard_map/ppermute | solution.py:763
  (34 other events, 402.0 us)
